TPU v7x, 256 devices: a whole 4x4x8 slice. The times are simulated.
256 devices in a mesh: ctx: 8 (over y, x_hi), dp: 16 (over x_lo, z), tp: 2 (over core).
Axes of the slice: x: 4 (x_hi: 2, x_lo: 2; x = x_hi * 2 + x_lo), y: 4, z: 8, core: 2. Of those that a mesh axis runs over, the one named last changes fastest.
Arguments:
- layer_input: bfloat16 [16, 2048, 8192], P('dp', 'ctx', 'tp'), may hold values from -6 to 6
- queries: bfloat16 [16, 2048, 4096], P('dp', 'ctx', 'tp'), may hold values from -64 to 64
- keys: bfloat16 [16, 2048, 512], P('dp', 'ctx', 'tp'), may hold values from -8 to 8
- values: bfloat16 [16, 2048, 512], P('dp', 'ctx', 'tp'), may hold values from -6 to 6
- out_grad: bfloat16 [16, 2048, 4096], P('dp', 'ctx', 'tp'), may hold values from -6 to 6
- doc_ids: int32 [16, 2048], P('dp', 'ctx'), may hold values from 0 to 3, never falling along the last dimension, each value on 1 to 1024 neighbouring positions
- freq_bins: int32 [64], replicated, may hold values from 0 to 32
- master: float32 [2, 4096, 512], P(None, 'dp', 'tp'), may hold values from -0.0625 to 0.0625
- moment1: float32 [2, 4096, 512], P(None, 'dp', 'tp'), may hold values from -3 to 3
- moment2: float32 [2, 4096, 512], P(None, 'dp', 'tp'), may hold values from 0.002 to 0.2
Outputs:
- query_grad: bfloat16 [16, 2048, 4096], P('dp', 'ctx', 'tp')
- value_grad: bfloat16 [16, 2048, 512], P('dp', 'ctx', 'tp')
- new_master: float32 [2, 4096, 512], P(None, 'dp', 'tp')
- new_moment1: float32 [2, 4096, 512], P(None, 'dp', 'tp')
- new_moment2: float32 [2, 4096, 512], P(None, 'dp', 'tp')
- key_weight: bfloat16 [2, 4096, 512], P(None, None, 'tp')
Inputs may be any that keep to these rules, and one draw needn't show every extreme that they name: `doc_ids`: each sequence holds 4 documents one after another, ids never falling along the sequence.
All inputs are finite; a program needn't handle non-finite values.
Results may differ from a plain program's by a relative error of at most 0.0079.
Values may be sent and summed in bfloat16 or wider, within the bound.
A program may use at most 128 MiB of HBM per device.

v0:
```python
import math

import jax
import jax.numpy as jnp
from jax import lax
from jax.sharding import PartitionSpec as P

HD = 128
BINS = 32
ADAM_STEP = 10


rope_base = 10000.0
yarn_factor = 8.0
magnitude_scale = 0.1 * math.log(8.0) + 1.0
beta_first = 0.9
beta_second = 0.95
adam_epsilon = 1e-08
learn_rate = 0.0003
weight_decay = 0.1


def frequencies(freq_bins):
    pairs = jnp.arange(HD // 2).astype(jnp.float32)
    theta = jnp.exp(pairs * (-2.0 * math.log(rope_base) / HD))
    gamma = freq_bins.astype(jnp.float32) / BINS
    return theta * ((1.0 - gamma) / yarn_factor + gamma)


def rotate(vectors, cosine, sine):
    half = vectors.shape[-1] // 2
    first = vectors[..., :half]
    second = vectors[..., half:]
    cosine = cosine[:, None, :]
    sine = sine[:, None, :]
    return jnp.concatenate(
        [first * cosine - second * sine, second * cosine + first * sine], axis=-1
    )


def unrotate(vectors, cosine, sine):
    half = vectors.shape[-1] // 2
    first = vectors[..., :half]
    second = vectors[..., half:]
    cosine = cosine[:, None, :]
    sine = sine[:, None, :]
    return jnp.concatenate(
        [first * cosine + second * sine, second * cosine - first * sine], axis=-1
    )


def on_device(
    layer_input, queries, keys, values, out_grad, doc_ids, freq_bins, master, moment1, moment2
):
    local_tokens = queries.shape[1]
    query_heads = queries.shape[2] // HD
    key_heads = keys.shape[2] // HD
    group_size = query_heads // key_heads
    ctx_count = lax.axis_size("ctx")
    data_count = lax.axis_size("dp")
    tp_count = lax.axis_size("tp")
    length = local_tokens * ctx_count
    inv_root = 1.0 / math.sqrt(HD)
    positions = lax.axis_index("ctx") * local_tokens + jnp.arange(local_tokens, dtype=jnp.int32)
    frequency = frequencies(freq_bins)
    angles = positions.astype(jnp.float32)[:, None] * frequency[None, :]
    cosine = jnp.cos(angles)
    sine = jnp.sin(angles)
    rot_q = (
        rotate(queries[0].reshape(local_tokens, query_heads, HD).astype(jnp.float32), cosine, sine)
        * magnitude_scale
    ).astype(jnp.bfloat16)
    rot_k = (
        rotate(keys[0].reshape(local_tokens, key_heads, HD).astype(jnp.float32), cosine, sine)
        * magnitude_scale
    ).astype(jnp.bfloat16)
    all_keys, all_values, all_docs = (
        lax.all_gather(rot_k.reshape(local_tokens, key_heads * HD), "ctx", axis=0, tiled=True),
        lax.all_gather(values[0], "ctx", axis=0, tiled=True),
        lax.all_gather(doc_ids[0], "ctx", axis=0, tiled=True),
    )
    key_positions = jnp.arange(length, dtype=jnp.int32)
    grad_heads = out_grad[0].reshape(local_tokens, query_heads, HD)
    query_rows = local_tokens * group_size
    block_rows = min(512, query_rows)
    block_count = query_rows // block_rows
    row_positions = jnp.repeat(positions, group_size).reshape(block_count, block_rows)
    row_docs = jnp.repeat(doc_ids[0], group_size).reshape(block_count, block_rows)
    contract_rows = (((0,), (0,)), ((), ()))
    query_parts = []
    key_parts = []
    value_parts = []
    for head in range(key_heads):
        query_block = rot_q[:, head * group_size : (head + 1) * group_size, :].reshape(
            block_count, block_rows, HD
        )
        grad_block = grad_heads[:, head * group_size : (head + 1) * group_size, :].reshape(
            block_count, block_rows, HD
        )
        key_head = all_keys[:, head * HD : (head + 1) * HD]
        value_head = all_values[:, head * HD : (head + 1) * HD]

        def one_block(carry, inputs):
            key_total, value_total = carry
            query_part, grad_part, pos_part, doc_part = inputs
            scores = (
                lax.dot_general(
                    query_part,
                    key_head,
                    (((1,), (1,)), ((), ())),
                    preferred_element_type=jnp.float32,
                )
                * inv_root
            )
            allowed = (key_positions[None, :] <= pos_part[:, None]) & (
                all_docs[None, :] == doc_part[:, None]
            )
            scores = jnp.where(allowed, scores, -jnp.inf)
            row_max = jnp.max(scores, axis=-1, keepdims=True)
            log_total = row_max + jnp.log(
                jnp.sum(jnp.exp(scores - row_max), axis=-1, keepdims=True)
            )
            probs = jnp.exp(scores - log_total)
            prob_grad = lax.dot_general(
                grad_part, value_head, (((1,), (1,)), ((), ())), preferred_element_type=jnp.float32
            )
            delta = jnp.sum(probs * prob_grad, axis=-1, keepdims=True)
            score_grad = (probs * (prob_grad - delta) * inv_root).astype(jnp.bfloat16)
            probs_bf = probs.astype(jnp.bfloat16)
            query_out = jnp.dot(score_grad, key_head, preferred_element_type=jnp.float32)
            key_total = key_total + lax.dot_general(
                score_grad, query_part, contract_rows, preferred_element_type=jnp.float32
            )
            value_total = value_total + lax.dot_general(
                probs_bf, grad_part, contract_rows, preferred_element_type=jnp.float32
            )
            return ((key_total, value_total), query_out)

        empty = jnp.zeros((length, HD), jnp.float32)
        (key_total, value_total), query_out = lax.scan(
            one_block, (empty, empty), (query_block, grad_block, row_positions, row_docs)
        )
        query_parts.append(query_out.reshape(local_tokens, group_size, HD))
        key_parts.append(key_total)
        value_parts.append(value_total)
    rot_q_grad = jnp.concatenate(query_parts, axis=1)
    key_terms = jnp.concatenate(key_parts, axis=1)
    value_terms = jnp.concatenate(value_parts, axis=1)
    key_sums, value_sums = (
        lax.psum_scatter(key_terms, "ctx", scatter_dimension=0, tiled=True),
        lax.psum_scatter(value_terms, "ctx", scatter_dimension=0, tiled=True),
    )
    query_grad = (
        (unrotate(rot_q_grad, cosine, sine) * magnitude_scale)
        .astype(jnp.bfloat16)
        .reshape(1, local_tokens, query_heads * HD)
    )
    value_grad = value_sums.astype(jnp.bfloat16).reshape(1, local_tokens, key_heads * HD)
    key_grad = (
        (unrotate(key_sums.reshape(local_tokens, key_heads, HD), cosine, sine) * magnitude_scale)
        .astype(jnp.bfloat16)
        .reshape(local_tokens, key_heads * HD)
    )
    gathered = lax.all_gather(layer_input[0], "tp", axis=1, tiled=True)
    group_rows = gathered.shape[1] // (tp_count * data_count)
    source = (
        gathered.reshape(local_tokens, tp_count, data_count, group_rows)
        .transpose(0, 2, 1, 3)
        .reshape(local_tokens, gathered.shape[1])
    )
    partial_sum = lax.psum_scatter(
        lax.dot_general(source, key_grad, contract_rows, preferred_element_type=jnp.float32),
        "dp",
        scatter_dimension=0,
        tiled=True,
    )
    gradient = lax.psum(partial_sum, "ctx")
    gradient = gradient * (1.0 / math.sqrt(data_count * length))
    gradient = gradient.reshape(tp_count, gradient.shape[0] // tp_count, gradient.shape[1])
    new_moment1 = beta_first * moment1 + (1.0 - beta_first) * gradient
    new_moment2 = beta_second * moment2 + (1.0 - beta_second) * gradient * gradient
    first_fix = 1.0 - beta_first**ADAM_STEP
    second_fix = 1.0 - beta_second**ADAM_STEP
    update = new_moment1 / first_fix / (jnp.sqrt(new_moment2 / second_fix) + adam_epsilon)
    new_master = master - learn_rate * (update + weight_decay * master)
    key_weight = lax.all_gather(new_master.astype(jnp.bfloat16), "dp", axis=1, tiled=True)
    return (query_grad, value_grad, new_master, new_moment1, new_moment2, key_weight)


def solution(mesh):
    placed = (
        P("dp", "ctx", "tp"),
        P("dp", "ctx", "tp"),
        P("dp", "ctx", "tp"),
        P("dp", "ctx", "tp"),
        P("dp", "ctx", "tp"),
        P("dp", "ctx"),
        P(),
        P(None, "dp", "tp"),
        P(None, "dp", "tp"),
        P(None, "dp", "tp"),
    )
    return jax.shard_map(
        on_device,
        mesh=mesh,
        in_specs=placed,
        out_specs=(
            P("dp", "ctx", "tp"),
            P("dp", "ctx", "tp"),
            P(None, "dp", "tp"),
            P(None, "dp", "tp"),
            P(None, "dp", "tp"),
            P(None, None, "tp"),
        ),
        check_vma=False,
    )
```

profile of v0, /device:TPU:8, one launch (start us, length us, event | category | flops | bytes accessed | tf_op | source)
XLA Modules:
  0.0 690.6 jit_solution(4289134766695654148)
XLA Ops:
  11.9 2.5 copy.22
  21.0 21.3 %all-gather = s32[1,2048]{1,0:T(1,128)S(1)} all-gather(s32[1,256]{1,0:T(1,128)S(1)} %copy-done.17), channel_id=2, replica_groups=mesh['ctx'=8,'dp'=16,'tp'=2] {'ctx'}, dimensions={1}, use_global_device_ids=true | all-gather | bytes 9216 | tf_op jit(solution)/shard_map/all_gather | solution.py:80
  43.8 20.8 %all-gather.12.cloned.1.call-done = bf16[1,2048,256]{2,1,0:T(8,128)(2,1)} async-done(((bf16[1,256,256]{2,1,0:T(8,128)(2,1)}), bf16[1,2048,256]{2,1,0:T(8,128)(2,1)}) %all-gather.12.cloned.1.call-update) | async-done | bytes 1048592 | tf_op jit(solution)/shard_map/all_gather | solution.py:79
  64.7 2.1 fusion.51
  66.8 51.4 %all-gather.8.cloned.1.call-done = bf16[2048,256]{1,0:T(8,128)(2,1)} async-done(((bf16[256,256]{1,0:T(8,128)(2,1)}), bf16[2048,256]{1,0:T(8,128)(2,1)}) %all-gather.8.cloned.1.call-update) | async-done | bytes 1048592 | tf_op jit(solution)/shard_map/all_gather | solution.py:78
  118.2 2.1 fusion.53
  121.3 54.4 %while.30 = (s32[]{:T(128)}, f32[2048,128]{1,0:T(8,128)}, f32[2048,128]{1,0:T(8,128)}, f32[4,512,128]{2,1,0:T(8,128)}, s32[4,512]{1,0:T(4,128)S(1)}, /*index=5*/...) while((s32[]{:T(128)}, f32[2048,128]{1,0:T(8,128)}, ...), condition=%wide.region_4.5_spmd.clone, body=%wide.region_0.4_spmd.clone.sunk | while | flops 1362099200 | bytes 92581816 | solution.py:140
  125.7 2.9 convolution_add_fusion.8
  128.5 2.5 fusion.95
  131.0 3.2 convolution_add_fusion.9
  138.8 3.3 convolution_add_fusion.8
  142.0 2.5 fusion.95
  144.5 3.6 convolution_add_fusion.9
  152.6 3.3 convolution_add_fusion.8
  155.8 2.4 fusion.95
  158.3 3.6 convolution_add_fusion.9
  166.4 3.3 convolution_add_fusion.8
  169.6 2.5 fusion.95
  172.1 3.6 convolution_add_fusion.9
  176.8 59.3 %while.31 = (s32[]{:T(128)}, f32[2048,128]{1,0:T(8,128)S(1)}, f32[2048,128]{1,0:T(8,128)}, f32[4,512,128]{2,1,0:T(8,128)}, s32[4,512]{1,0:T(4,128)S(1)}, /*index...) while((s32[]{:T(128)}, f32[2048,128]{1,0:T(8,128)S(1)}, ...), condition=%wide.region_9.10_spmd.clone, body=%wide.region_5.9_spmd.clone.sunk | while | flops 1362099200 | bytes 77902560 | solution.py:140
  176.8 2.4 fusion.104
  183.7 2.1 convolution_add_fusion.10
  185.8 2.5 fusion.105
  188.3 3.0 convolution_add_fusion.11
  191.3 2.4 fusion.104
  198.2 2.1 convolution_add_fusion.10
  200.3 2.5 fusion.105
  202.8 3.4 convolution_add_fusion.11
  206.2 2.4 fusion.104
  210.0 2.0 multiply_reduce_fusion.5
  213.1 2.1 convolution_add_fusion.10
  215.3 2.5 fusion.105
  217.7 3.4 convolution_add_fusion.11
  221.2 2.4 fusion.104
  228.1 2.1 convolution_add_fusion.10
  230.2 2.5 fusion.105
  232.7 3.4 convolution_add_fusion.11
  236.1 2.8 pad_maximum_fusion.2
  238.9 4.6 copy.23
  243.6 74.3 %reduce-scatter.6.cloned.1.call-done = f32[256,256]{1,0:T(8,128)} async-done(((f32[2048,256]{1,0:T(8,128)}), f32[256,256]{1,0:T(8,128)}) %reduce-scatter.6.cloned.1.call-update) | async-done | bytes 262160 | tf_op jit(solution)/shard_map/reduce_scatter | solution.py:150
  319.9 6.8 convolution_bitcast_fusion.2
  326.7 100.4 %reduce-scatter.8.cloned.1.call-done = f32[512,256]{0,1:T(8,128)} async-done(((f32[8192,256]{0,1:T(8,128)}), f32[512,256]{0,1:T(8,128)}) %reduce-scatter.8.cloned.1.call-update) | async-done | bytes 524304 | tf_op jit(solution)/shard_map/reduce_scatter | solution.py:171
  427.2 3.0 pad_maximum_fusion.1
  430.3 86.8 %all-reduce.2.cloned.1.call-done = f32[512,256]{0,1:T(8,128)} async-done(((f32[512,256]{0,1:T(8,128)}), f32[512,256]{0,1:T(8,128)}) %all-reduce.2.cloned.1.call-update) | async-done | bytes 524304 | tf_op jit(solution)/shard_map/psum | solution.py:177
  518.4 3.0 fusion.47
  524.2 77.1 %reduce-scatter.4.cloned.1.call-done = f32[256,256]{1,0:T(8,128)} async-done(((f32[2048,256]{1,0:T(8,128)}), f32[256,256]{1,0:T(8,128)}) %reduce-scatter.4.cloned.1.call-update) | async-done | bytes 262160 | tf_op jit(solution)/shard_map/reduce_scatter | solution.py:151
  602.9 76.4 %all-gather.10.cloned.1.call-done = bf16[2,4096,256]{2,1,0:T(8,128)(2,1)} async-done(((bf16[2,256,256]{2,1,0:T(8,128)(2,1)}), bf16[2,4096,256]{2,1,0:T(8,128)(2,1)}) %all-gather.10.cloned.1.call-update) | async-done | bytes 4194320 | tf_op jit(solution)/shard_map/all_gather | solution.py:186
  679.3 4.5 copy.66
  (211 shorter events, 56.2 us)
Async XLA Ops:
  7.2 4.7 copy-start.15
  7.2 57.5 %all-gather.12.cloned.1.call-start = ((), (), s32[]{:S(2)}) async-start(), calls=%async_computation.9 | async-start | bytes 1179648 | tf_op jit(solution)/shard_map/all_gather | solution.py:79
  7.9 110.2 %all-gather.8.cloned.1.call-start = ((), (), s32[]{:S(2)}) async-start(), calls=%async_computation.3 | async-start | bytes 1179648 | tf_op jit(solution)/shard_map/all_gather | solution.py:78
  11.8 227.1 %all-gather.14.cloned.1.call-start = ((), (), s32[]{:S(2)}) async-start(), calls=%async_computation.10 | async-start | bytes 6291456 | tf_op jit(solution)/shard_map/all_gather | solution.py:164
  14.4 303.5 %reduce-scatter.6.cloned.1.call-start = ((), (), s32[]{:S(2)}) async-start(), calls=%async_computation.5 | async-start | bytes 2359296 | tf_op jit(solution)/shard_map/reduce_scatter | solution.py:150
  18.6 2.3 copy-start.17
  121.3 2.0 copy-start.5
  121.3 2.0 copy-start.9
  125.7 5.4 copy-start.1
  131.0 3.3 copy-start.6
  131.0 3.3 copy-start.8
  131.0 3.3 copy-start.10
  131.0 3.3 copy-start.14
  134.3 2.0 copy-start.5
  134.3 2.0 copy-start.9
  138.7 5.7 copy-start.1
  144.5 3.6 copy-start.6
  144.5 3.6 copy-start.8
  144.5 3.6 copy-start.10
  144.5 3.6 copy-start.14
  148.1 2.0 copy-start.5
  148.1 2.0 copy-start.9
  152.5 5.7 copy-start.1
  158.3 3.6 copy-start.6
  158.3 3.6 copy-start.8
  158.3 3.6 copy-start.10
  158.3 3.6 copy-start.14
  161.9 2.0 copy-start.5
  161.9 2.0 copy-start.9
  166.3 5.7 copy-start.1
  172.1 3.6 copy-start.6
  172.1 3.6 copy-start.8
  172.1 3.6 copy-start.10
  172.1 3.6 copy-start.14
  179.1 3.5 copy-start.2
  183.7 4.6 copy-start.3
  193.7 3.5 copy-start.2
  198.2 4.6 copy-start.3
  208.6 3.5 copy-start.2
  213.1 4.6 copy-start.3
  223.5 3.5 copy-start.2
  228.1 4.6 copy-start.3
  238.9 188.3 %reduce-scatter.8.cloned.1.call-start = ((), (), s32[]{:S(2)}) async-start(), calls=%async_computation.6 | async-start | bytes 8912896 | tf_op jit(solution)/shard_map/reduce_scatter | solution.py:171
  326.7 190.4 %all-reduce.2.cloned.1.call-start = ((), (), s32[]{:S(2)}) async-start(), calls=%async_computation.7 | async-start | bytes 1048576 | tf_op jit(solution)/shard_map/psum | solution.py:177
  427.2 174.1 %reduce-scatter.4.cloned.1.call-start = ((), (), s32[]{:S(2)}) async-start(), calls=%async_computation.4 | async-start | bytes 2359296 | tf_op jit(solution)/shard_map/reduce_scatter | solution.py:151
  430.2 249.1 %all-gather.10.cloned.1.call-start = ((), (), s32[]{:S(2)}) async-start(), calls=%async_computation.8 | async-start | bytes 4456448 | tf_op jit(solution)/shard_map/all_gather | solution.py:186
  518.4 3.0 copy-start.11
  518.4 3.0 copy-start.12
  (17 other events, 25.4 us)
Sparse Core Ops, SparseCore 0:
  10.7 53.9 all-gather.11
  67.9 50.2 all-gather.7
  120.0 18.1 all-gather.13
  239.0 78.8 reduce-scatter.5
  326.8 100.2 reduce-scatter.7
  429.6 87.4 all-reduce.1
  522.2 79.0 reduce-scatter.3
  603.2 76.0 all-gather.9
where the time goes:
time: 692 us; the launch traced here: 691 us
  waiting for transfers between devices  488 us (71%)
  matrix products  101 us (15%)
  other arithmetic  32.4 us (5%)
  local copies, waits for them, and re-layouts  31.9 us (5%)
  blocking collectives  21.3 us (3%)
  between operations  14.4 us (2%)
    reduce_scatter x1, waiting for transfers between devices, on_device(): lax.psum_scatter(lax.dot_general(source, key_grad, contract_rows, preferr...  100 us
    psum x1, waiting for transfers between devices, on_device(): gradient = lax.psum(partial_sum, 'ctx')  86.8 us
    reduce_scatter x1, waiting for transfers between devices, on_device(): lax.psum_scatter(value_terms, 'ctx', scatter_dimension=0, tiled=True)  77.1 us
    all_gather x1, waiting for transfers between devices, on_device(): lax.all_gather(new_master.astype(jnp.bfloat16), 'dp', axis=1, tiled=True)  76.4 us
    reduce_scatter x1, waiting for transfers between devices, on_device(): lax.psum_scatter(key_terms, 'ctx', scatter_dimension=0, tiled=True)  74.3 us
    all_gather x1, waiting for transfers between devices, on_device(): lax.all_gather(rot_k.reshape(local_tokens, key_heads * HD), 'ctx', axis=0...  51.4 us
    dot_general x8, matrix products, one_block(): lax.dot_general(probs_bf, grad_part, contract_rows, preferred_element_typ...  27.3 us
    all_gather x1, blocking collectives, on_device(): lax.all_gather(doc_ids[0], 'ctx', axis=0, tiled=True)  21.3 us
  transfers between devices with their start and end apart: 8, of which 7 were waited for; matrix products, arithmetic and copies ran while one was open for 21% of the time, Pallas kernels for 0%

commit v1 on v0

v1 whole, which is shorter than its diff:
```python
import functools
import math

import jax
import jax.numpy as jnp
from jax import lax
from jax.experimental import pallas as pl
from jax.experimental.pallas import tpu as pltpu
from jax.sharding import PartitionSpec as P

HD = 128
BINS = 32
ADAM_STEP = 10
NCTX = 8
NDP = 16
NZ = 8
NPLANE = 16
BACK = 4
LOC = 256
GROUP = 8
KVH = 2
WIN = (BACK + 1) * LOC
CH = 128

rope_base = 10000.0
yarn_factor = 8.0
magnitude_scale = 0.1 * math.log(8.0) + 1.0
beta_first = 0.9
beta_second = 0.95
adam_epsilon = 1e-08
learn_rate = 0.0003
weight_decay = 0.1
inv_root = 1.0 / math.sqrt(HD)
MESH = pl.DeviceIdType.MESH
F32 = jnp.float32
BF16 = jnp.bfloat16


def frequencies(freq_bins):
    pairs = jnp.arange(HD // 2).astype(jnp.float32)
    theta = jnp.exp(pairs * (-2.0 * math.log(rope_base) / HD))
    gamma = freq_bins.astype(jnp.float32) / BINS
    return theta * ((1.0 - gamma) / yarn_factor + gamma)


def dot_nt(a, b):
    return lax.dot_general(a, b, (((1,), (1,)), ((), ())), preferred_element_type=F32)


def dot_nn(a, b):
    return lax.dot_general(a, b, (((1,), (0,)), ((), ())), preferred_element_type=F32)


def rows8(op, value):
    return op(value.reshape(value.shape[0] // 8, 8, value.shape[1]), axis=0)


def kernel(
    q_hbm, og_hbm, k_ref, v_ref, doc_ref, cos_ref, sin_ref, x_hbm, ms_hbm, m1_hbm, m2_hbm,
    dq_hbm, dv_out, nms_out, nm1_out, nm2_out, kw_hbm,
    q_v, og_v, dq_v, kv, kt, docs, bias, t_ref, dp_ref, p_ref, ds_ref, dk_acc, dv_acc,
    term_send, term_recv, kg_own, dv_own, xr, kgt, gtb, rbuf, gall, opt_v, wb,
    local_sem, doc_send_sem, doc_recv_sem, kv_send_sem, kv_recv_sem, x_send_sem, x_recv_sem,
    xf_send_sem, xf_recv_sem, term_send_sem, term_recv_sem, kg_send_sem, kg_recv_sem,
    rs_send_sem, rs_recv_sem, ga_send_sem, ga_recv_sem,
    sw_send_sem, sw_recv_sem, ring_send_sem, ring_recv_sem,
    zs_send_sem, zs_recv_sem, pl_send_sem, pl_recv_sem,
):
    c = lax.axis_index("ctx")
    d = lax.axis_index("dp")
    t = lax.axis_index("tp")
    z = lax.rem(d, NZ)
    xl = d // NZ
    me_p = xl * NCTX + c

    def z_peer(k):
        return (c, xl * NZ + lax.rem(z + k, NZ), t)

    def plane_peer(k):
        p = lax.rem(me_p + k, NPLANE)
        return p, (lax.rem(p, NCTX), (p // NCTX) * NZ + z, t)

    def ctx_peer(k):
        return (lax.rem(c + k, NCTX), d, t)

    def remote(src, dst, ssem, rsem, device):
        return pltpu.make_async_remote_copy(
            src_ref=src, dst_ref=dst, send_sem=ssem, recv_sem=rsem,
            device_id=device, device_id_type=MESH,
        )

    q_copy = pltpu.make_async_copy(q_hbm, q_v, local_sem.at[0])
    og_copy = pltpu.make_async_copy(og_hbm, og_v, local_sem.at[1])
    opt_copies = [
        pltpu.make_async_copy(src, opt_v.at[i], local_sem.at[2 + i])
        for i, src in enumerate((ms_hbm, m1_hbm, m2_hbm))
    ]
    x_own = [
        pltpu.make_async_copy(
            x_hbm.at[:, pl.ds(pl.multiple_of((i * NZ + z) * LOC, LOC), LOC)],
            xr.at[t, i, pl.ds(pl.multiple_of(z * LOC, LOC), LOC), :],
            local_sem.at[5 + i],
        )
        for i in range(2)
    ]
    for copy in [q_copy, og_copy] + opt_copies + x_own:
        copy.start()

    barrier = pltpu.get_barrier_semaphore()

    def greet_z(k, carry):
        pl.semaphore_signal(barrier, inc=1, device_id=z_peer(k), device_id_type=MESH)
        return carry

    def greet_plane(k, carry):
        pl.semaphore_signal(barrier, inc=1, device_id=plane_peer(k)[1], device_id_type=MESH)
        return carry

    lax.fori_loop(1, NZ, greet_z, 0)
    lax.fori_loop(1, NPLANE, greet_plane, 0)
    pl.semaphore_signal(barrier, inc=1, device_id=(c, d, 1 - t), device_id_type=MESH)

    cosv = cos_ref[...]
    sinv = sin_ref[...]
    for g in range(KVH):
        kh = k_ref[:, g * HD:(g + 1) * HD].astype(F32)
        kv[g, 0, 0:LOC, :] = (kh * cosv + pltpu.roll(kh, HD // 2, 1) * sinv).astype(BF16)
        kv[g, 1, 0:LOC, :] = v_ref[:, g * HD:(g + 1) * HD]
    docs[0] = jnp.broadcast_to(doc_ref[...], (8, LOC))

    pl.semaphore_wait(barrier, (NZ - 1) + (NPLANE - 1) + 1)

    def doc_copy(k):
        return remote(docs.at[0], docs.at[k], doc_send_sem.at[k - 1], doc_recv_sem.at[k - 1], ctx_peer(k))

    def kv_copy(g, k):
        return remote(
            kv.at[g, :, pl.ds(0, LOC), :], kv.at[g, :, pl.ds(k * LOC, LOC), :],
            kv_send_sem.at[g, k - 1], kv_recv_sem.at[g, k - 1], ctx_peer(k),
        )

    for k in range(1, BACK + 1):
        @pl.when(c + k < NCTX)
        def _(k=k):
            doc_copy(k).start()
            kv_copy(0, k).start()

    def x_copy(k, i):
        zd = lax.rem(z + k, NZ)
        return remote(
            x_hbm.at[:, pl.ds(pl.multiple_of((i * NZ + zd) * LOC, LOC), LOC)],
            xr.at[t, i, pl.ds(pl.multiple_of(z * LOC, LOC), LOC), :],
            x_send_sem.at[k, i], x_recv_sem.at[k, i], z_peer(k),
        )

    def x_start(k, carry):
        x_copy(k, 0).start()
        x_copy(k, 1).start()
        return carry

    lax.fori_loop(1, NZ, x_start, 0)

    for k in range(1, BACK + 1):
        @pl.when(c + k < NCTX)
        def _(k=k):
            kv_copy(1, k).start()

        @pl.when(c < k)
        def _(k=k):
            kv[:, :, k * LOC:(k + 1) * LOC, :] = jnp.zeros((KVH, 2, LOC, HD), BF16)
            docs[k] = jnp.full((8, LOC), 127, jnp.int32)

    for k in range(1, BACK + 1):
        @pl.when(c >= k)
        def _(k=k):
            doc_copy(k).wait_recv()
    own_docs = doc_ref[...]
    window_start = jnp.maximum(c - BACK, 0) * LOC
    start = jnp.zeros((1, LOC), F32)
    for doc in range(1, 4):
        below = jnp.zeros((8, LOC), F32)
        for k in range(BACK + 1):
            below = below + (docs[k] < doc).astype(F32)
        count = jnp.sum(below[0:1], axis=1, keepdims=True)
        start = jnp.where(own_docs == doc, count, start)
    start = start.astype(jnp.int32) + window_start
    query_pos = c * LOC + lax.broadcasted_iota(jnp.int32, (1, LOC), 1)
    for k in range(BACK + 1):
        key_pos = (c - k) * LOC + lax.broadcasted_iota(jnp.int32, (LOC, LOC), 0)
        seen = (key_pos <= query_pos) & (key_pos >= start)
        bias[k * LOC:(k + 1) * LOC, :] = jnp.where(seen, 0.0, -jnp.inf)

    q_copy.wait()
    og_copy.wait()
    scale2 = inv_root * math.log2(math.e)
    chunks = [slice(j * CH, (j + 1) * CH) for j in range(WIN // CH)]

    def term_copy(g, kind, k):
        return remote(
            term_send.at[g, kind, k - 1], term_recv.at[g, kind, k - 1],
            term_send_sem.at[g, kind, k - 1], term_recv_sem.at[g, kind, k - 1],
            ctx_peer(NCTX - k),
        )

    for g in range(KVH):
        for k in range(1, BACK + 1):
            @pl.when(c >= k)
            def _(k=k, g=g):
                kv_copy(g, k).wait_recv()
        for sl in chunks:
            kt[:, sl] = kv[g, 0, sl, :].astype(F32).T.astype(BF16)
        dk_acc[...] = jnp.zeros_like(dk_acc)
        dv_acc[...] = jnp.zeros_like(dv_acc)

        def one_head(h, carry, g=g):
            col = pl.ds(pl.multiple_of((g * GROUP + h) * HD, HD), HD)
            qh = q_v[:, col].astype(F32)
            rq = (qh * cos_ref[...] + pltpu.roll(qh, HD // 2, 1) * sin_ref[...]).astype(BF16)
            do = og_v[:, col]
            top = None
            for sl in chunks:
                score = dot_nt(kv[g, 0, sl, :], rq) * scale2 + bias[sl, :]
                t_ref[sl, :] = score
                part = rows8(jnp.max, score)
                top = part if top is None else jnp.maximum(top, part)
            top = jnp.max(top, axis=0, keepdims=True)
            total = jnp.zeros((8, LOC), F32)
            mixed = jnp.zeros((8, LOC), F32)
            for sl in chunks:
                e = jnp.exp2(t_ref[sl, :] - top)
                t_ref[sl, :] = e
                dp = dot_nt(kv[g, 1, sl, :], do)
                dp_ref[sl, :] = dp
                total = total + rows8(jnp.sum, e)
                mixed = mixed + rows8(jnp.sum, e * dp)
            inv_total = 1.0 / jnp.sum(total, axis=0, keepdims=True)
            delta = jnp.sum(mixed, axis=0, keepdims=True) * inv_total
            for sl in chunks:
                p = t_ref[sl, :] * inv_total
                ds = (p * (dp_ref[sl, :] - delta)).astype(BF16)
                ds_ref[sl, :] = ds
                dk_acc[sl, :] += dot_nn(ds, rq)
                dv_acc[sl, :] += dot_nn(p.astype(BF16), do)
            dq = dot_nn(kt[...], ds_ref[...]).T * inv_root
            dq_v[:, col] = (dq * cos_ref[...] - pltpu.roll(dq, HD // 2, 1) * sin_ref[...]).astype(BF16)
            return carry

        lax.fori_loop(0, GROUP, one_head, 0)

        kg_own[g] = dk_acc[0:LOC, :] * inv_root
        dv_own[g] = dv_acc[0:LOC, :]
        for k in range(1, BACK + 1):
            rows = slice(k * LOC, (k + 1) * LOC)
            term_send[g, 0, k - 1] = (dk_acc[rows, :] * inv_root).astype(BF16)
            term_send[g, 1, k - 1] = dv_acc[rows, :].astype(BF16)
        for kind in range(2):
            for k in range(1, BACK + 1):
                @pl.when(c >= k)
                def _(k=k, g=g, kind=kind):
                    term_copy(g, kind, k).start()

    dq_copy = pltpu.make_async_copy(dq_v, dq_hbm, local_sem.at[7])
    dq_copy.start()

    def kg_copy(g, k):
        part = kgt.at[z, pl.ds(g * HD, HD), :]
        return remote(part, part, kg_send_sem.at[g, k], kg_recv_sem.at[g, k], z_peer(k))

    for g in range(KVH):
        for k in range(1, BACK + 1):
            @pl.when(c + k < NCTX)
            def _(k=k, g=g):
                term_copy(g, 0, k).wait_recv()
                kg_own[g] = kg_own[g] + term_recv[g, 0, k - 1].astype(F32)
        kg = kg_own[g]
        kg = kg * cosv - pltpu.roll(kg, HD // 2, 1) * sinv
        kgt[z, pl.ds(g * HD, HD), :] = kg.T.astype(BF16)

        def kg_start(k, carry, g=g):
            kg_copy(g, k).start()
            return carry

        lax.fori_loop(1, NZ, kg_start, 0)

    for copy in x_own:
        copy.wait()

    def x_wait(k, carry):
        x_copy(k, 0).wait_recv()
        x_copy(k, 1).wait_recv()
        return carry

    lax.fori_loop(1, NZ, x_wait, 0)
    xf_copy = remote(xr.at[t], xr.at[t], xf_send_sem, xf_recv_sem, (c, d, 1 - t))
    xf_copy.start()

    for g in range(KVH):
        for k in range(1, BACK + 1):
            @pl.when(c + k < NCTX)
            def _(k=k, g=g):
                term_copy(g, 1, k).wait_recv()
                dv_own[g] = dv_own[g] + term_recv[g, 1, k - 1].astype(F32)
        dv_out[:, g * HD:(g + 1) * HD] = dv_own[g].astype(BF16)

    def kg_wait(k, carry):
        kg_copy(0, k).wait_recv()
        kg_copy(1, k).wait_recv()
        return carry

    lax.fori_loop(1, NZ, kg_wait, 0)
    xf_copy.wait_recv()

    for i in range(2):
        for h in range(2):
            acc = jnp.zeros((LOC, LOC), F32)
            for s in range(NZ):
                acc = acc + dot_nn(kgt[s], xr[h, i, s * LOC:(s + 1) * LOC, :])
            gtb[i, :, h * LOC:(h + 1) * LOC] = acc.astype(BF16)

    part_rows = LOC // NCTX

    def rs_copy(k):
        p, device = plane_peer(k)
        return remote(
            gtb.at[p // NCTX, pl.ds(pl.multiple_of(lax.rem(p, NCTX) * part_rows, part_rows), part_rows), :],
            rbuf.at[k], rs_send_sem.at[k], rs_recv_sem.at[k], device,
        )

    def rs_start(k, carry):
        rs_copy(k).start()
        return carry

    lax.fori_loop(1, NPLANE, rs_start, 0)

    def rs_sum(k, total):
        rs_copy(k).wait_recv()
        return total + rbuf[k].astype(F32)

    own_rows = pl.ds(pl.multiple_of(c * part_rows, part_rows), part_rows)
    total = lax.fori_loop(1, NPLANE, rs_sum, gtb[xl, own_rows, :].astype(F32))
    gall[own_rows, :] = (total * (1.0 / math.sqrt(NDP * NCTX * LOC))).astype(BF16)

    def ga_copy(k):
        return remote(gall.at[own_rows, :], gall.at[own_rows, :], ga_send_sem.at[k], ga_recv_sem.at[k], ctx_peer(k))

    def ga_start(k, carry):
        ga_copy(k).start()
        return carry

    def ga_wait(k, carry):
        ga_copy(k).wait_recv()
        return carry

    lax.fori_loop(1, NCTX, ga_start, 0)
    for copy in opt_copies:
        copy.wait()
    lax.fori_loop(1, NCTX, ga_wait, 0)

    first_fix = 1.0 - beta_first**ADAM_STEP
    second_fix = 1.0 - beta_second**ADAM_STEP
    for h in range(2):
        grad = gall[:, h * LOC:(h + 1) * LOC].astype(F32).T
        nm1 = beta_first * opt_v[1, h] + (1.0 - beta_first) * grad
        nm2 = beta_second * opt_v[2, h] + (1.0 - beta_second) * grad * grad
        update = nm1 / first_fix / (jnp.sqrt(nm2 / second_fix) + adam_epsilon)
        nms = opt_v[0, h] - learn_rate * (update + weight_decay * opt_v[0, h])
        nms_out[h] = nms
        nm1_out[h] = nm1
        nm2_out[h] = nm2
        wb[h] = nms.astype(BF16).reshape(NCTX, part_rows, LOC)

    keeps = [
        pltpu.make_async_copy(wb.at[0], kw_hbm.at[0, d], local_sem.at[8]),
        pltpu.make_async_copy(wb.at[1, c], kw_hbm.at[1, d, c], local_sem.at[9]),
    ]
    for keep in keeps:
        keep.start()

    def zs_copy(k):
        return remote(
            wb.at[1, c], kw_hbm.at[1, d, c], zs_send_sem.at[k], zs_recv_sem.at[k], z_peer(k),
        )

    swap = remote(wb.at[0], kw_hbm.at[0, d], sw_send_sem, sw_recv_sem, (c, (1 - xl) * NZ + z, t))

    def ring_copy(s, way, same, src=None):
        step = 1 if way == 0 else NZ - 1
        zb = lax.rem(z + (NZ - s if way == 0 else s), NZ)
        block = (xl if same else 1 - xl) * NZ + zb
        return remote(
            kw_hbm.at[0, block] if src is None else src, kw_hbm.at[0, block],
            ring_send_sem.at[way, s, int(same)], ring_recv_sem.at[way, s, int(same)], z_peer(step),
        )

    def zs_start(k, carry):
        zs_copy(k).start()
        return carry

    swap.start()
    ring_copy(0, 0, True, wb.at[0]).start()
    ring_copy(0, 1, True, wb.at[0]).start()
    lax.fori_loop(1, NZ, zs_start, 0)

    def zs_wait(k, carry):
        zs_copy(k).wait_recv()
        return carry

    swap.wait_recv()
    ring_copy(0, 0, False).start()
    ring_copy(0, 1, False).start()
    lax.fori_loop(1, NZ, zs_wait, 0)
    for keep in keeps:
        keep.wait()

    def pl_copy(k):
        device = plane_peer(k)[1]
        part = kw_hbm.at[1, pl.ds(xl * NZ, NZ), c]
        return remote(part, part, pl_send_sem.at[k], pl_recv_sem.at[k], device)

    def pl_start(k, carry):
        pl_copy(k).start()
        return carry

    lax.fori_loop(1, NPLANE, pl_start, 0)

    ring = [(s, way, same) for s in range(4) for same in (True, False) for way in range(2) if s < 3 or same == (way == 0)]
    for s, way, same in ring:
        ring_copy(s, way, same).wait_recv()
        if (s + 1, way, same) in ring:
            ring_copy(s + 1, way, same).start()

    def pl_wait(k, carry):
        pl_copy(k).wait_recv()
        return carry

    lax.fori_loop(1, NPLANE, pl_wait, 0)

    for k in range(1, BACK + 1):
        @pl.when(c + k < NCTX)
        def _(k=k):
            doc_copy(k).wait_send()
            for g in range(KVH):
                kv_copy(g, k).wait_send()

        @pl.when(c >= k)
        def _(k=k):
            for g in range(KVH):
                for kind in range(2):
                    term_copy(g, kind, k).wait_send()

    def z_sent(k, carry):
        x_copy(k, 0).wait_send()
        x_copy(k, 1).wait_send()
        kg_copy(0, k).wait_send()
        kg_copy(1, k).wait_send()
        zs_copy(k).wait_send()
        return carry

    lax.fori_loop(1, NZ, z_sent, 0)

    def plane_sent(k, carry):
        rs_copy(k).wait_send()
        pl_copy(k).wait_send()
        return carry

    lax.fori_loop(1, NPLANE, plane_sent, 0)

    def ctx_sent(k, carry):
        ga_copy(k).wait_send()
        return carry

    lax.fori_loop(1, NCTX, ctx_sent, 0)
    xf_copy.wait_send()
    swap.wait_send()
    for s, way, same in ring:
        ring_copy(s, way, same).wait_send()
    dq_copy.wait()


def on_device(
    layer_input, queries, keys, values, out_grad, doc_ids, freq_bins, master, moment1, moment2
):
    positions = lax.axis_index("ctx") * LOC + jnp.arange(LOC, dtype=jnp.int32)
    angles = positions.astype(F32)[:, None] * frequencies(freq_bins)[None, :]
    cosine = jnp.cos(angles) * magnitude_scale
    sine = jnp.sin(angles) * magnitude_scale
    cosine = jnp.concatenate([cosine, cosine], axis=1)
    sine = jnp.concatenate([-sine, sine], axis=1)

    any_ = pl.BlockSpec(memory_space=pl.ANY)
    vmem = pl.BlockSpec(memory_space=pltpu.VMEM)
    dma = pltpu.SemaphoreType.DMA
    part_rows = LOC // NCTX
    rows, cols = 2, LOC
    state = jax.ShapeDtypeStruct((rows, LOC, cols), F32)
    dq, dv, nms, nm1, nm2, kw = pl.pallas_call(
        kernel,
        out_shape=(
            jax.ShapeDtypeStruct((LOC, KVH * GROUP * HD), BF16),
            jax.ShapeDtypeStruct((LOC, KVH * HD), BF16),
            state, state, state,
            jax.ShapeDtypeStruct((2, NDP, NCTX, part_rows, cols), BF16),
        ),
        in_specs=[any_, any_, vmem, vmem, vmem, vmem, vmem, any_, any_, any_, any_],
        out_specs=(any_, vmem, vmem, vmem, vmem, any_),
        scratch_shapes=[
            pltpu.VMEM((LOC, KVH * GROUP * HD), BF16),
            pltpu.VMEM((LOC, KVH * GROUP * HD), BF16),
            pltpu.VMEM((LOC, KVH * GROUP * HD), BF16),
            pltpu.VMEM((KVH, 2, WIN, HD), BF16),
            pltpu.VMEM((HD, WIN), BF16),
            pltpu.VMEM((BACK + 1, 8, LOC), jnp.int32),
            pltpu.VMEM((WIN, LOC), F32),
            pltpu.VMEM((WIN, LOC), F32),
            pltpu.VMEM((WIN, LOC), F32),
            pltpu.VMEM((WIN, LOC), BF16),
            pltpu.VMEM((WIN, LOC), BF16),
            pltpu.VMEM((WIN, HD), F32),
            pltpu.VMEM((WIN, HD), F32),
            pltpu.VMEM((KVH, 2, BACK, LOC, HD), BF16),
            pltpu.VMEM((KVH, 2, BACK, LOC, HD), BF16),
            pltpu.VMEM((KVH, LOC, HD), F32),
            pltpu.VMEM((KVH, LOC, HD), F32),
            pltpu.VMEM((2, 2, NZ * LOC, LOC), BF16),
            pltpu.VMEM((NZ, LOC, LOC), BF16),
            pltpu.VMEM((2, LOC, 2 * LOC), BF16),
            pltpu.VMEM((NPLANE, part_rows, 2 * LOC), BF16),
            pltpu.VMEM((LOC, 2 * LOC), BF16),
            pltpu.VMEM((3, 2, LOC, LOC), F32),
            pltpu.VMEM((2, NCTX, part_rows, LOC), BF16),
            dma((10,)),
            dma((BACK,)), dma((BACK,)),
            dma((KVH, BACK)), dma((KVH, BACK)),
            dma((NZ, 2)), dma((NZ, 2)),
            dma, dma,
            dma((KVH, 2, BACK)), dma((KVH, 2, BACK)),
            dma((KVH, NZ)), dma((KVH, NZ)),
            dma((NPLANE,)), dma((NPLANE,)),
            dma((NCTX,)), dma((NCTX,)),
            dma, dma,
            dma((2, 4, 2)), dma((2, 4, 2)),
            dma((NZ,)), dma((NZ,)),
            dma((NPLANE,)), dma((NPLANE,)),
        ],
        compiler_params=pltpu.CompilerParams(
            collective_id=0, has_side_effects=True, vmem_limit_bytes=48 * 1024 * 1024
        ),
    )(
        queries[0], out_grad[0], keys[0], values[0], doc_ids, cosine, sine, layer_input[0],
        master, moment1, moment2,
    )
    return (dq[None], dv[None], nms, nm1, nm2, kw.reshape(2, NDP * LOC, cols))


def solution(mesh):
    placed = (
        P("dp", "ctx", "tp"),
        P("dp", "ctx", "tp"),
        P("dp", "ctx", "tp"),
        P("dp", "ctx", "tp"),
        P("dp", "ctx", "tp"),
        P("dp", "ctx"),
        P(),
        P(None, "dp", "tp"),
        P(None, "dp", "tp"),
        P(None, "dp", "tp"),
    )
    return jax.shard_map(
        on_device,
        mesh=mesh,
        in_specs=placed,
        out_specs=(
            P("dp", "ctx", "tp"),
            P("dp", "ctx", "tp"),
            P(None, "dp", "tp"),
            P(None, "dp", "tp"),
            P(None, "dp", "tp"),
            P(None, None, "tp"),
        ),
        check_vma=False,
    )
```

time: 692 us -> 147 us (0.21)
  waiting for transfers between devices: 488 us -> 0 us
  Pallas kernels: 0 us -> 131 us
  matrix products: 101 us -> 0 us
  other arithmetic: 32.4 us -> 1.35 us
  blocking collectives: 21.3 us -> 0 us
  local copies, waits for them, and re-layouts: 31.9 us -> 12.9 us
  between operations: 14.4 us -> 0.69 us
    reduce_scatter x3 -> x0, waiting for transfers between devices: 252 us -> none  [the longest x1 100 us: on_device(): lax.psum_scatter(lax.dot_general(source, key_grad, contract_rows, preferr...]
    all_gather x4 -> x0, waiting for transfers between devices: 149 us -> none  [the longest x1 76.4 us: on_device(): lax.all_gather(new_master.astype(jnp.bfloat16), 'dp', axis=1, tiled=True)]
    pallas_call x0 -> x1, Pallas kernels: none -> 131 us  [on_device(): pl.pallas_call(kernel, out_shape=(jax.ShapeDtypeStruct((LOC, KVH * GROUP...]
    dot_general x41 -> x0, matrix products: 101 us -> none  [the longest x8 27.3 us: one_block(): lax.dot_general(probs_bf, grad_part, contract_rows, preferred_element_typ...]
    psum x1 -> x0, waiting for transfers between devices: 86.8 us -> none  [on_device(): gradient = lax.psum(partial_sum, 'ctx')]
    all_gather x1 -> x0, blocking collectives: 21.3 us -> none  [on_device(): lax.all_gather(doc_ids[0], 'ctx', axis=0, tiled=True)]
    convert_element_type x14 -> x1, other arithmetic: 13.5 us -> 0.01 us  [on_device(): angles = positions.astype(F32)[:, None] * frequencies(freq_bins)[None, :]]
  transfers between devices with their start and end apart: 8 -> 0, of which waited for: 7 -> 0; matrix products, arithmetic and copies ran while one was open for 21% -> 0% of each run, Pallas kernels for 0% -> 0%
where the time goes in v1:
time: 147 us; the launch traced here: 146 us
  Pallas kernels  131 us (89%)
  local copies, waits for them, and re-layouts  12.9 us (9%)
    pallas_call x1, Pallas kernels, on_device(): pl.pallas_call(kernel, out_shape=(jax.ShapeDtypeStruct((LOC, KVH * GROUP...  131 us
    unnamed x22, local copies, waits for them, and re-layouts  12.9 us

profile of v1, /device:TPU:8, one launch (start us, length us, event | category | flops | bytes accessed | tf_op | source)
XLA Modules:
  0.0 145.8 jit_solution(9406411508854118955)
XLA Ops:
  0.6 0.7 add_multiply_fusion
  1.3 0.6 fusion.2
  1.9 0.1 pad_maximum_fusion
  2.0 0.0 copy-start
  2.0 1.2 copy-done
  3.2 0.0 copy-start.1
  3.2 1.0 copy-done.1
  4.3 0.0 copy-start.2
  4.3 1.0 copy-done.2
  5.3 0.0 copy-start.3
  5.3 1.0 copy-done.3
  6.4 0.0 copy-start.4
  6.4 0.9 copy-done.4
  7.3 0.0 copy-start.5
  7.3 0.9 copy-done.5
  8.2 0.0 copy-start.6
  8.2 0.7 copy-done.6
  8.8 130.9 %shard_map.145 = (bf16[256,2048]{1,0:T(8,128)(2,1)S(1)}, bf16[256,256]{1,0:T(8,128)(2,1)S(1)}, f32[2,256,256]{2,1,0:T(8,128)S(1)}, f32[2,256,256]{2,1,0:T(8,128)...) custom-call(bf16[256,2048]{1,0:T(8,128)(2,1)S(1)} %bitcast.9, bf16[256,2048]{1,0:T(8,128)(2,1)} %bitcast.15, ...), custom_call_target="tpu_custom_call" | custom-call | tf_op jit(solution)/shard_map/pallas_call | solution.py:496
  139.7 0.0 copy-start.7
  139.8 1.0 copy.22
  140.7 0.7 copy.23
  141.4 0.8 copy.24
  142.2 0.8 copy.25
  143.0 0.8 copy.26
  143.8 0.0 copy-done.7
  143.8 2.0 %copy.27 = bf16[2,4096,256]{2,1,0:T(8,128)(2,1)} copy(bf16[2,4096,256]{2,1,0:T(8,128)(2,1)S(1)} %bitcast.13) | data formatting | bytes 8388608
  (1 shorter events, 0.0 us)
Async XLA Ops:
  2.0 1.2 copy-start
  3.2 1.0 copy-start.1
  4.3 1.0 copy-start.2
  5.3 1.0 copy-start.3
  6.4 0.9 copy-start.4
  7.3 0.9 copy-start.5
  8.2 0.7 copy-start.6
  139.7 4.0 %copy-start.7 = (bf16[2,16,8,32,256]{4,3,2,1,0:T(8,128)(2,1)S(1)}, bf16[2,16,8,32,256]{4,3,2,1,0:T(8,128)(2,1)}, u32[]{:S(2)}) copy-start(bf16[2,16,8,32,256]{4,3,2,1,0:T(8,128)(2,1)} %get-tuple-element.17) | copy-start | bytes 12582916

commit v2 on v1

--- a/solution.py
+++ b/solution.py
@@ -51,14 +51,23 @@
     return lax.dot_general(a, b, (((1,), (0,)), ((), ())), preferred_element_type=F32)
 
 
+def adam(grad, master, moment1, moment2):
+    new_moment1 = beta_first * moment1 + (1.0 - beta_first) * grad
+    new_moment2 = beta_second * moment2 + (1.0 - beta_second) * grad * grad
+    first_fix = 1.0 - beta_first**ADAM_STEP
+    second_fix = 1.0 - beta_second**ADAM_STEP
+    update = new_moment1 / first_fix / (jnp.sqrt(new_moment2 / second_fix) + adam_epsilon)
+    return master - learn_rate * (update + weight_decay * master), new_moment1, new_moment2
+
+
 def rows8(op, value):
     return op(value.reshape(value.shape[0] // 8, 8, value.shape[1]), axis=0)
 
 
 def kernel(
     q_hbm, og_hbm, k_ref, v_ref, doc_ref, cos_ref, sin_ref, x_hbm, ms_hbm, m1_hbm, m2_hbm,
-    dq_hbm, dv_out, nms_out, nm1_out, nm2_out, kw_hbm,
-    q_v, og_v, dq_v, kv, kt, docs, bias, t_ref, dp_ref, p_ref, ds_ref, dk_acc, dv_acc,
+    dq_hbm, dv_out, grad_out, kw_hbm,
+    q_v, og_v, dq_v, kv, kt, docs, bias, rq_ref, t_ref, dp_ref, p_ref, ds_ref, dk_acc, dv_acc,
     term_send, term_recv, kg_own, dv_own, xr, kgt, gtb, rbuf, gall, opt_v, wb,
     local_sem, doc_send_sem, doc_recv_sem, kv_send_sem, kv_recv_sem, x_send_sem, x_recv_sem,
     xf_send_sem, xf_recv_sem, term_send_sem, term_recv_sem, kg_send_sem, kg_recv_sem,
@@ -89,6 +98,15 @@
             device_id=device, device_id_type=MESH,
         )
 
+    sent = []
+
+    def over(low, high, one):
+        def step(k, carry):
+            one(k)
+            return carry
+
+        lax.fori_loop(low, high, step, 0)
+
     q_copy = pltpu.make_async_copy(q_hbm, q_v, local_sem.at[0])
     og_copy = pltpu.make_async_copy(og_hbm, og_v, local_sem.at[1])
     opt_copies = [
@@ -145,6 +163,16 @@
             doc_copy(k).start()
             kv_copy(0, k).start()
 
+    def kv_sent():
+        for k in range(1, BACK + 1):
+            @pl.when(c + k < NCTX)
+            def _(k=k):
+                doc_copy(k).wait_send()
+                for g in range(KVH):
+                    kv_copy(g, k).wait_send()
+
+    sent.append(kv_sent)
+
     def x_copy(k, i):
         zd = lax.rem(z + k, NZ)
         return remote(
@@ -157,6 +185,12 @@
         x_copy(k, 0).start()
         x_copy(k, 1).start()
         return carry
+
+    def x_sent(k):
+        x_copy(k, 0).wait_send()
+        x_copy(k, 1).wait_send()
+
+    sent.append(lambda: over(1, NZ, x_sent))
 
     lax.fori_loop(1, NZ, x_start, 0)
 
@@ -202,6 +236,15 @@
             ctx_peer(NCTX - k),
         )
 
+    def term_sent(g):
+        for k in range(1, BACK + 1):
+            @pl.when(c >= k)
+            def _(k=k):
+                for kind in range(2):
+                    term_copy(g, kind, k).wait_send()
+
+    sent.append(lambda: term_sent(0))
+    sent.append(lambda: term_sent(1))
     for g in range(KVH):
         for k in range(1, BACK + 1):
             @pl.when(c >= k)
@@ -212,40 +255,55 @@
         dk_acc[...] = jnp.zeros_like(dk_acc)
         dv_acc[...] = jnp.zeros_like(dv_acc)
 
-        def one_head(h, carry, g=g):
-            col = pl.ds(pl.multiple_of((g * GROUP + h) * HD, HD), HD)
-            qh = q_v[:, col].astype(F32)
+        def head_columns(h, g=g):
+            return pl.ds(pl.multiple_of((g * GROUP + h) * HD, HD), HD)
+
+        def products(h, b, g=g):
+            qh = q_v[:, head_columns(h)].astype(F32)
             rq = (qh * cos_ref[...] + pltpu.roll(qh, HD // 2, 1) * sin_ref[...]).astype(BF16)
-            do = og_v[:, col]
+            rq_ref[b] = rq
+            t_ref[b] = dot_nt(kv[g, 0], rq)
+            dp_ref[b] = dot_nt(kv[g, 1], og_v[:, head_columns(h)])
+
+        def softmax(b):
             top = None
             for sl in chunks:
-                score = dot_nt(kv[g, 0, sl, :], rq) * scale2 + bias[sl, :]
-                t_ref[sl, :] = score
+                score = t_ref[b, sl, :] * scale2 + bias[sl, :]
+                t_ref[b, sl, :] = score
                 part = rows8(jnp.max, score)
                 top = part if top is None else jnp.maximum(top, part)
             top = jnp.max(top, axis=0, keepdims=True)
             total = jnp.zeros((8, LOC), F32)
             mixed = jnp.zeros((8, LOC), F32)
             for sl in chunks:
-                e = jnp.exp2(t_ref[sl, :] - top)
-                t_ref[sl, :] = e
-                dp = dot_nt(kv[g, 1, sl, :], do)
-                dp_ref[sl, :] = dp
+                e = jnp.exp2(t_ref[b, sl, :] - top)
+                t_ref[b, sl, :] = e
                 total = total + rows8(jnp.sum, e)
-                mixed = mixed + rows8(jnp.sum, e * dp)
+                mixed = mixed + rows8(jnp.sum, e * dp_ref[b, sl, :])
             inv_total = 1.0 / jnp.sum(total, axis=0, keepdims=True)
             delta = jnp.sum(mixed, axis=0, keepdims=True) * inv_total
             for sl in chunks:
-                p = t_ref[sl, :] * inv_total
-                ds = (p * (dp_ref[sl, :] - delta)).astype(BF16)
-                ds_ref[sl, :] = ds
-                dk_acc[sl, :] += dot_nn(ds, rq)
-                dv_acc[sl, :] += dot_nn(p.astype(BF16), do)
-            dq = dot_nn(kt[...], ds_ref[...]).T * inv_root
-            dq_v[:, col] = (dq * cos_ref[...] - pltpu.roll(dq, HD // 2, 1) * sin_ref[...]).astype(BF16)
+                p = t_ref[b, sl, :] * inv_total
+                ds_ref[b, sl, :] = (p * (dp_ref[b, sl, :] - delta)).astype(BF16)
+                p_ref[b, sl, :] = p.astype(BF16)
+
+        def gradients(h, b):
+            dk_acc[...] += dot_nn(ds_ref[b], rq_ref[b])
+            dv_acc[...] += dot_nn(p_ref[b], og_v[:, head_columns(h)])
+            dq = dot_nn(kt[...], ds_ref[b]).T * inv_root
+            dq = dq * cos_ref[...] - pltpu.roll(dq, HD // 2, 1) * sin_ref[...]
+            dq_v[:, head_columns(h)] = dq.astype(BF16)
+
+        def two_heads(i, carry):
+            for b in range(2):
+                products(2 * i + b, b)
+            for b in range(2):
+                softmax(b)
+            for b in range(2):
+                gradients(2 * i + b, b)
             return carry
 
-        lax.fori_loop(0, GROUP, one_head, 0)
+        lax.fori_loop(0, GROUP // 2, two_heads, 0)
 
         kg_own[g] = dk_acc[0:LOC, :] * inv_root
         dv_own[g] = dv_acc[0:LOC, :]
@@ -261,11 +319,17 @@
 
     dq_copy = pltpu.make_async_copy(dq_v, dq_hbm, local_sem.at[7])
     dq_copy.start()
-
-    def kg_copy(g, k):
-        part = kgt.at[z, pl.ds(g * HD, HD), :]
-        return remote(part, part, kg_send_sem.at[g, k], kg_recv_sem.at[g, k], z_peer(k))
-
+    sent.append(dq_copy.wait)
+
+    def kg_copy(s, way, g):
+        zb = lax.rem(z + (NZ - s if way == 0 else s), NZ)
+        part = kgt.at[zb, pl.ds(g * HD, HD), :]
+        return remote(
+            part, part, kg_send_sem.at[way, s, g], kg_recv_sem.at[way, s, g],
+            z_peer(1 if way == 0 else NZ - 1),
+        )
+
+    kg_ring = [(s, way, g) for s in range(4) for g in range(KVH) for way in range(2) if s < 3 or g == way]
     for g in range(KVH):
         for k in range(1, BACK + 1):
             @pl.when(c + k < NCTX)
@@ -275,24 +339,33 @@
         kg = kg_own[g]
         kg = kg * cosv - pltpu.roll(kg, HD // 2, 1) * sinv
         kgt[z, pl.ds(g * HD, HD), :] = kg.T.astype(BF16)
-
-        def kg_start(k, carry, g=g):
-            kg_copy(g, k).start()
-            return carry
-
-        lax.fori_loop(1, NZ, kg_start, 0)
-
-    for copy in x_own:
-        copy.wait()
-
-    def x_wait(k, carry):
-        x_copy(k, 0).wait_recv()
-        x_copy(k, 1).wait_recv()
-        return carry
-
-    lax.fori_loop(1, NZ, x_wait, 0)
-    xf_copy = remote(xr.at[t], xr.at[t], xf_send_sem, xf_recv_sem, (c, d, 1 - t))
-    xf_copy.start()
+        for way in range(2):
+            kg_copy(0, way, g).start()
+
+    def xf_copy(k):
+        rows = pl.ds(pl.multiple_of(lax.rem(z + NZ - k, NZ) * LOC, LOC), LOC)
+        part = xr.at[t, :, rows, :]
+        return remote(part, part, xf_send_sem.at[k], xf_recv_sem.at[k], (c, d, 1 - t))
+
+    def x_forward(k):
+        if k == 0:
+            for copy in x_own:
+                copy.wait()
+        else:
+            x_copy(k, 0).wait_recv()
+            x_copy(k, 1).wait_recv()
+        xf_copy(k).start()
+
+    for k in (0, 1, 7, 2, 6):
+        x_forward(k)
+    for s, way, g in kg_ring:
+        kg_copy(s, way, g).wait_recv()
+        if (s + 1, way, g) in kg_ring:
+            kg_copy(s + 1, way, g).start()
+    for k in (3, 5, 4):
+        x_forward(k)
+    sent.extend(kg_copy(s, way, g).wait_send for s, way, g in kg_ring)
+    sent.append(lambda: over(0, NZ, lambda k: xf_copy(k).wait_send()))
 
     for g in range(KVH):
         for k in range(1, BACK + 1):
@@ -302,13 +375,10 @@
                 dv_own[g] = dv_own[g] + term_recv[g, 1, k - 1].astype(F32)
         dv_out[:, g * HD:(g + 1) * HD] = dv_own[g].astype(BF16)
 
-    def kg_wait(k, carry):
-        kg_copy(0, k).wait_recv()
-        kg_copy(1, k).wait_recv()
-        return carry
-
-    lax.fori_loop(1, NZ, kg_wait, 0)
-    xf_copy.wait_recv()
+    def xf_wait(k):
+        xf_copy(k).wait_recv()
+
+    over(0, NZ, xf_wait)
 
     for i in range(2):
         for h in range(2):
@@ -336,6 +406,7 @@
         rs_copy(k).wait_recv()
         return total + rbuf[k].astype(F32)
 
+    sent.append(lambda: over(1, NPLANE, lambda k: rs_copy(k).wait_send()))
     own_rows = pl.ds(pl.multiple_of(c * part_rows, part_rows), part_rows)
     total = lax.fori_loop(1, NPLANE, rs_sum, gtb[xl, own_rows, :].astype(F32))
     gall[own_rows, :] = (total * (1.0 / math.sqrt(NDP * NCTX * LOC))).astype(BF16)
@@ -356,17 +427,11 @@
         copy.wait()
     lax.fori_loop(1, NCTX, ga_wait, 0)
 
-    first_fix = 1.0 - beta_first**ADAM_STEP
-    second_fix = 1.0 - beta_second**ADAM_STEP
+    sent.append(lambda: over(1, NCTX, lambda k: ga_copy(k).wait_send()))
     for h in range(2):
         grad = gall[:, h * LOC:(h + 1) * LOC].astype(F32).T
-        nm1 = beta_first * opt_v[1, h] + (1.0 - beta_first) * grad
-        nm2 = beta_second * opt_v[2, h] + (1.0 - beta_second) * grad * grad
-        update = nm1 / first_fix / (jnp.sqrt(nm2 / second_fix) + adam_epsilon)
-        nms = opt_v[0, h] - learn_rate * (update + weight_decay * opt_v[0, h])
-        nms_out[h] = nms
-        nm1_out[h] = nm1
-        nm2_out[h] = nm2
+        grad_out[h] = grad
+        nms = adam(grad, opt_v[0, h], opt_v[1, h], opt_v[2, h])[0]
         wb[h] = nms.astype(BF16).reshape(NCTX, part_rows, LOC)
 
     keeps = [
@@ -396,6 +461,8 @@
         zs_copy(k).start()
         return carry
 
+    sent.append(swap.wait_send)
+    sent.append(lambda: over(1, NZ, lambda k: zs_copy(k).wait_send()))
     swap.start()
     ring_copy(0, 0, True, wb.at[0]).start()
     ring_copy(0, 1, True, wb.at[0]).start()
@@ -423,58 +490,23 @@
 
     lax.fori_loop(1, NPLANE, pl_start, 0)
 
+    sent.append(lambda: over(1, NPLANE, lambda k: pl_copy(k).wait_send()))
     ring = [(s, way, same) for s in range(4) for same in (True, False) for way in range(2) if s < 3 or same == (way == 0)]
     for s, way, same in ring:
         ring_copy(s, way, same).wait_recv()
         if (s + 1, way, same) in ring:
             ring_copy(s + 1, way, same).start()
 
+    sent.extend(ring_copy(s, way, same).wait_send for s, way, same in ring)
+
     def pl_wait(k, carry):
         pl_copy(k).wait_recv()
         return carry
 
     lax.fori_loop(1, NPLANE, pl_wait, 0)
 
-    for k in range(1, BACK + 1):
-        @pl.when(c + k < NCTX)
-        def _(k=k):
-            doc_copy(k).wait_send()
-            for g in range(KVH):
-                kv_copy(g, k).wait_send()
-
-        @pl.when(c >= k)
-        def _(k=k):
-            for g in range(KVH):
-                for kind in range(2):
-                    term_copy(g, kind, k).wait_send()
-
-    def z_sent(k, carry):
-        x_copy(k, 0).wait_send()
-        x_copy(k, 1).wait_send()
-        kg_copy(0, k).wait_send()
-        kg_copy(1, k).wait_send()
-        zs_copy(k).wait_send()
-        return carry
-
-    lax.fori_loop(1, NZ, z_sent, 0)
-
-    def plane_sent(k, carry):
-        rs_copy(k).wait_send()
-        pl_copy(k).wait_send()
-        return carry
-
-    lax.fori_loop(1, NPLANE, plane_sent, 0)
-
-    def ctx_sent(k, carry):
-        ga_copy(k).wait_send()
-        return carry
-
-    lax.fori_loop(1, NCTX, ctx_sent, 0)
-    xf_copy.wait_send()
-    swap.wait_send()
-    for s, way, same in ring:
-        ring_copy(s, way, same).wait_send()
-    dq_copy.wait()
+    for wait in sent:
+        wait()
 
 
 def on_device(
@@ -492,17 +524,16 @@
     dma = pltpu.SemaphoreType.DMA
     part_rows = LOC // NCTX
     rows, cols = 2, LOC
-    state = jax.ShapeDtypeStruct((rows, LOC, cols), F32)
-    dq, dv, nms, nm1, nm2, kw = pl.pallas_call(
+    dq, dv, grad, kw = pl.pallas_call(
         kernel,
         out_shape=(
             jax.ShapeDtypeStruct((LOC, KVH * GROUP * HD), BF16),
             jax.ShapeDtypeStruct((LOC, KVH * HD), BF16),
-            state, state, state,
+            jax.ShapeDtypeStruct((rows, LOC, cols), F32),
             jax.ShapeDtypeStruct((2, NDP, NCTX, part_rows, cols), BF16),
         ),
         in_specs=[any_, any_, vmem, vmem, vmem, vmem, vmem, any_, any_, any_, any_],
-        out_specs=(any_, vmem, vmem, vmem, vmem, any_),
+        out_specs=(any_, vmem, vmem, any_),
         scratch_shapes=[
             pltpu.VMEM((LOC, KVH * GROUP * HD), BF16),
             pltpu.VMEM((LOC, KVH * GROUP * HD), BF16),
@@ -511,10 +542,11 @@
             pltpu.VMEM((HD, WIN), BF16),
             pltpu.VMEM((BACK + 1, 8, LOC), jnp.int32),
             pltpu.VMEM((WIN, LOC), F32),
-            pltpu.VMEM((WIN, LOC), F32),
-            pltpu.VMEM((WIN, LOC), F32),
-            pltpu.VMEM((WIN, LOC), BF16),
-            pltpu.VMEM((WIN, LOC), BF16),
+            pltpu.VMEM((2, LOC, HD), BF16),
+            pltpu.VMEM((2, WIN, LOC), F32),
+            pltpu.VMEM((2, WIN, LOC), F32),
+            pltpu.VMEM((2, WIN, LOC), BF16),
+            pltpu.VMEM((2, WIN, LOC), BF16),
             pltpu.VMEM((WIN, HD), F32),
             pltpu.VMEM((WIN, HD), F32),
             pltpu.VMEM((KVH, 2, BACK, LOC, HD), BF16),
@@ -532,9 +564,9 @@
             dma((BACK,)), dma((BACK,)),
             dma((KVH, BACK)), dma((KVH, BACK)),
             dma((NZ, 2)), dma((NZ, 2)),
-            dma, dma,
+            dma((NZ,)), dma((NZ,)),
             dma((KVH, 2, BACK)), dma((KVH, 2, BACK)),
-            dma((KVH, NZ)), dma((KVH, NZ)),
+            dma((2, 4, KVH)), dma((2, 4, KVH)),
             dma((NPLANE,)), dma((NPLANE,)),
             dma((NCTX,)), dma((NCTX,)),
             dma, dma,
@@ -543,13 +575,14 @@
             dma((NPLANE,)), dma((NPLANE,)),
         ],
         compiler_params=pltpu.CompilerParams(
-            collective_id=0, has_side_effects=True, vmem_limit_bytes=48 * 1024 * 1024
+            collective_id=0, has_side_effects=True, vmem_limit_bytes=54 * 1024 * 1024
         ),
     )(
         queries[0], out_grad[0], keys[0], values[0], doc_ids, cosine, sine, layer_input[0],
         master, moment1, moment2,
     )
-    return (dq[None], dv[None], nms, nm1, nm2, kw.reshape(2, NDP * LOC, cols))
+    new_master, new_moment1, new_moment2 = adam(grad, master, moment1, moment2)
+    return (dq[None], dv[None], new_master, new_moment1, new_moment2, kw.reshape(2, NDP * LOC, cols))
 
 
 def solution(mesh):

time: 147 us -> 142 us (0.966)
  local copies, waits for them, and re-layouts: 12.9 us -> 5 us
  other arithmetic: 1.35 us -> 4.74 us
    unnamed x22 -> x13, local copies, waits for them, and re-layouts: 12.9 us -> 5 us
    sub x0 -> x1, other arithmetic: none -> 2.57 us  [adam(): master - learn_rate * (update + weight_decay * master)]
where the time goes in v2:
time: 142 us; the launch traced here: 140 us
  Pallas kernels  130 us (92%)
  local copies, waits for them, and re-layouts  5 us (4%)
  other arithmetic  4.74 us (3%)
    pallas_call x1, Pallas kernels, on_device(): pl.pallas_call(kernel, out_shape=(jax.ShapeDtypeStruct((LOC, KVH * GROUP...  130 us
    unnamed x13, local copies, waits for them, and re-layouts  5 us

profile of v2, /device:TPU:8, one launch (start us, length us, event | category | flops | bytes accessed | tf_op | source)
XLA Modules:
  0.0 140.3 jit_solution(11360451581214535283)
XLA Ops:
  0.6 0.0 copy-start.3
  0.6 0.0 copy-start.2
  0.7 0.0 copy-start.1
  0.7 0.8 add_multiply_fusion
  1.5 0.6 fusion.3
  2.0 0.8 pad_maximum_fusion
  2.9 129.8 %shard_map.145 = (bf16[256,2048]{1,0:T(8,128)(2,1)}, bf16[256,256]{1,0:T(8,128)(2,1)}, f32[2,256,256]{2,1,0:T(8,128)}, bf16[2,16,8,32,256]{4,3,2,1,0:T(8,128)(2,1)}) custom-call(bf16[256,2048]{1,0:T(8,128)(2,1)} %bitcast.11, bf16[256,2048]{1,0:T(8,128)(2,1)} %bitcast.12, bf16[256,256]{1,0:T(8,128)(2,1)} %bitcast.14, bf16[256,256]{1,0:T(8,128)(2,1)} %bitcast.15, ...), custom_call_target="tpu_custom_call" | custom-call | tf_op jit(solution)/shard_map/pallas_call | solution.py:527
  132.7 0.0 copy-start.4
  132.7 0.0 copy-start
  132.7 0.0 copy-done.3
  132.7 0.0 copy-done.2
  132.7 0.0 copy-done.1
  132.8 2.6 %multiply_subtract_fusion = (f32[2,256,256]{2,1,0:T(8,128)}, f32[2,256,256]{2,1,0:T(8,128)}, f32[2,256,256]{2,1,0:T(8,128)}) fusion(f32[2,256,256]{2,1,0:T(8,128)S(1)} %copy-done.1, f32[2,256,256]{2,1,0:T(8,128)} %get-tuple-element.12, f32[2,256,256]{2,1,0:T(8,128)S(1)} %copy-done.2, f32[2,256,256]{2,1,0:T(8,128)S(1)} %copy-done.3), kind=kLoop, calls=%fused_computation.2 | loop fusion | flops 1966080 | bytes 3670016 | tf_op jit(solution)/shard_map/sub | solution.py:60
  135.3 2.3 %copy.19 = bf16[1,256,2048]{2,1,0:T(8,128)(2,1)} copy(bf16[1,256,2048]{2,1,0:T(8,128)(2,1)} %bitcast.10) | data formatting | bytes 2097152
  137.6 0.0 copy-done.4
  137.6 0.7 copy.20
  138.3 0.0 copy-done
  138.3 2.0 %copy.21 = bf16[2,4096,256]{2,1,0:T(8,128)(2,1)} copy(bf16[2,4096,256]{2,1,0:T(8,128)(2,1)S(1)} %bitcast.8) | data formatting | bytes 8388608
  (1 shorter events, 0.0 us)
Async XLA Ops:
  0.6 132.1 %copy-start.3 = (f32[2,256,256]{2,1,0:T(8,128)S(1)}, f32[2,256,256]{2,1,0:T(8,128)}, u32[]{:S(2)}) copy-start(f32[2,256,256]{2,1,0:T(8,128)} %m2_hbm.1) | copy-start | bytes 1572868
  0.6 132.1 %copy-start.2 = (f32[2,256,256]{2,1,0:T(8,128)S(1)}, f32[2,256,256]{2,1,0:T(8,128)}, u32[]{:S(2)}) copy-start(f32[2,256,256]{2,1,0:T(8,128)} %m1_hbm.1) | copy-start | bytes 1572868
  0.7 132.1 %copy-start.1 = (f32[2,256,256]{2,1,0:T(8,128)S(1)}, f32[2,256,256]{2,1,0:T(8,128)}, u32[]{:S(2)}) copy-start(f32[2,256,256]{2,1,0:T(8,128)} %ms_hbm.1) | copy-start | bytes 1572868
  132.7 4.9 %copy-start.4 = (bf16[256,256]{1,0:T(8,128)(2,1)S(1)}, bf16[256,256]{1,0:T(8,128)(2,1)}, u32[]{:S(2)}) copy-start(bf16[256,256]{1,0:T(8,128)(2,1)} %get-tuple-element.11) | copy-start | bytes 393220
  132.7 5.6 %copy-start = (bf16[2,16,8,32,256]{4,3,2,1,0:T(8,128)(2,1)S(1)}, bf16[2,16,8,32,256]{4,3,2,1,0:T(8,128)(2,1)}, u32[]{:S(2)}) copy-start(bf16[2,16,8,32,256]{4,3,2,1,0:T(8,128)(2,1)} %get-tuple-element.13) | copy-start | bytes 12582916

commit v3 on v2

--- a/solution.py
+++ b/solution.py
@@ -68,7 +68,7 @@
     q_hbm, og_hbm, k_ref, v_ref, doc_ref, cos_ref, sin_ref, x_hbm, ms_hbm, m1_hbm, m2_hbm,
     dq_hbm, dv_out, grad_out, kw_hbm,
     q_v, og_v, dq_v, kv, kt, docs, bias, rq_ref, t_ref, dp_ref, p_ref, ds_ref, dk_acc, dv_acc,
-    term_send, term_recv, kg_own, dv_own, xr, kgt, gtb, rbuf, gall, opt_v, wb,
+    term_send, term_recv, kg_own, dv_own, xr, kgt, gacc, gtb, rbuf, gall, opt_v, wb,
     local_sem, doc_send_sem, doc_recv_sem, kv_send_sem, kv_recv_sem, x_send_sem, x_recv_sem,
     xf_send_sem, xf_recv_sem, term_send_sem, term_recv_sem, kg_send_sem, kg_recv_sem,
     rs_send_sem, rs_recv_sem, ga_send_sem, ga_recv_sem,
@@ -356,17 +356,6 @@
             x_copy(k, 1).wait_recv()
         xf_copy(k).start()
 
-    for k in (0, 1, 7, 2, 6):
-        x_forward(k)
-    for s, way, g in kg_ring:
-        kg_copy(s, way, g).wait_recv()
-        if (s + 1, way, g) in kg_ring:
-            kg_copy(s + 1, way, g).start()
-    for k in (3, 5, 4):
-        x_forward(k)
-    sent.extend(kg_copy(s, way, g).wait_send for s, way, g in kg_ring)
-    sent.append(lambda: over(0, NZ, lambda k: xf_copy(k).wait_send()))
-
     for g in range(KVH):
         for k in range(1, BACK + 1):
             @pl.when(c + k < NCTX)
@@ -375,17 +364,31 @@
                 dv_own[g] = dv_own[g] + term_recv[g, 1, k - 1].astype(F32)
         dv_out[:, g * HD:(g + 1) * HD] = dv_own[g].astype(BF16)
 
-    def xf_wait(k):
+    for s, way, g in kg_ring:
+        kg_copy(s, way, g).wait_recv()
+        if (s + 1, way, g) in kg_ring:
+            kg_copy(s + 1, way, g).start()
+    sources = (0, 1, 7, 2, 6, 3, 5, 4)
+    x_forward(sources[0])
+    sent.extend(kg_copy(s, way, g).wait_send for s, way, g in kg_ring)
+    sent.append(lambda: over(0, NZ, lambda k: xf_copy(k).wait_send()))
+
+    for n, k in enumerate(sources):
+        if n + 1 < NZ:
+            x_forward(sources[n + 1])
         xf_copy(k).wait_recv()
-
-    over(0, NZ, xf_wait)
-
-    for i in range(2):
-        for h in range(2):
-            acc = jnp.zeros((LOC, LOC), F32)
-            for s in range(NZ):
-                acc = acc + dot_nn(kgt[s], xr[h, i, s * LOC:(s + 1) * LOC, :])
-            gtb[i, :, h * LOC:(h + 1) * LOC] = acc.astype(BF16)
+        source = lax.rem(z + NZ - k, NZ)
+        tokens = pl.ds(pl.multiple_of(source * LOC, LOC), LOC)
+        for i in range(2):
+            for h in range(2):
+                rows = slice(h * LOC, (h + 1) * LOC)
+                term = dot_nn(kgt[source], xr[h, i, tokens, :])
+                if n > 0:
+                    term = term + gacc[i, :, rows]
+                if n + 1 < NZ:
+                    gacc[i, :, rows] = term
+                else:
+                    gtb[i, :, rows] = term.astype(BF16)
 
     part_rows = LOC // NCTX
 
@@ -555,6 +558,7 @@
             pltpu.VMEM((KVH, LOC, HD), F32),
             pltpu.VMEM((2, 2, NZ * LOC, LOC), BF16),
             pltpu.VMEM((NZ, LOC, LOC), BF16),
+            pltpu.VMEM((2, LOC, 2 * LOC), F32),
             pltpu.VMEM((2, LOC, 2 * LOC), BF16),
             pltpu.VMEM((NPLANE, part_rows, 2 * LOC), BF16),
             pltpu.VMEM((LOC, 2 * LOC), BF16),

time: 142 us -> 143 us (level)
  Pallas kernels: 130 us -> 132 us
    pallas_call x1, Pallas kernels: 130 us -> 132 us  [on_device(): pl.pallas_call(kernel, out_shape=(jax.ShapeDtypeStruct((LOC, KVH * GROUP...]
where the time goes in v3:
time: 143 us; the launch traced here: 142 us
  Pallas kernels  132 us (92%)
  local copies, waits for them, and re-layouts  5 us (3%)
  other arithmetic  4.74 us (3%)
    pallas_call x1, Pallas kernels, on_device(): pl.pallas_call(kernel, out_shape=(jax.ShapeDtypeStruct((LOC, KVH * GROUP...  132 us
    unnamed x13, local copies, waits for them, and re-layouts  5 us

profile of v3, /device:TPU:8, one launch (start us, length us, event | category | flops | bytes accessed | tf_op | source)
XLA Modules:
  0.0 142.0 jit_solution(11454462718305161765)
XLA Ops:
  0.6 0.0 copy-start.3
  0.6 0.0 copy-start.2
  0.7 0.0 copy-start.1
  0.7 0.8 add_multiply_fusion
  1.5 0.6 fusion.3
  2.0 0.8 pad_maximum_fusion
  2.9 131.6 %shard_map.145 = (bf16[256,2048]{1,0:T(8,128)(2,1)}, bf16[256,256]{1,0:T(8,128)(2,1)}, f32[2,256,256]{2,1,0:T(8,128)}, bf16[2,16,8,32,256]{4,3,2,1,0:T(8,128)(2,1)}) custom-call(bf16[256,2048]{1,0:T(8,128)(2,1)} %bitcast.11, bf16[256,2048]{1,0:T(8,128)(2,1)} %bitcast.12, bf16[256,256]{1,0:T(8,128)(2,1)} %bitcast.14, bf16[256,256]{1,0:T(8,128)(2,1)} %bitcast.15, ...), custom_call_target="tpu_custom_call" | custom-call | tf_op jit(solution)/shard_map/pallas_call | solution.py:530
  134.4 0.0 copy-start.4
  134.4 0.0 copy-start
  134.4 0.0 copy-done.3
  134.4 0.0 copy-done.2
  134.5 0.0 copy-done.1
  134.5 2.6 %multiply_subtract_fusion = (f32[2,256,256]{2,1,0:T(8,128)}, f32[2,256,256]{2,1,0:T(8,128)}, f32[2,256,256]{2,1,0:T(8,128)}) fusion(f32[2,256,256]{2,1,0:T(8,128)S(1)} %copy-done.1, f32[2,256,256]{2,1,0:T(8,128)} %get-tuple-element.12, f32[2,256,256]{2,1,0:T(8,128)S(1)} %copy-done.2, f32[2,256,256]{2,1,0:T(8,128)S(1)} %copy-done.3), kind=kLoop, calls=%fused_computation.2 | loop fusion | flops 1966080 | bytes 3670016 | tf_op jit(solution)/shard_map/sub | solution.py:60
  137.0 2.3 %copy.19 = bf16[1,256,2048]{2,1,0:T(8,128)(2,1)} copy(bf16[1,256,2048]{2,1,0:T(8,128)(2,1)} %bitcast.10) | data formatting | bytes 2097152
  139.3 0.0 copy-done.4
  139.3 0.7 copy.20
  140.0 0.0 copy-done
  140.0 2.0 %copy.21 = bf16[2,4096,256]{2,1,0:T(8,128)(2,1)} copy(bf16[2,4096,256]{2,1,0:T(8,128)(2,1)S(1)} %bitcast.8) | data formatting | bytes 8388608
  (1 shorter events, 0.0 us)
Async XLA Ops:
  0.6 133.8 %copy-start.3 = (f32[2,256,256]{2,1,0:T(8,128)S(1)}, f32[2,256,256]{2,1,0:T(8,128)}, u32[]{:S(2)}) copy-start(f32[2,256,256]{2,1,0:T(8,128)} %m2_hbm.1) | copy-start | bytes 1572868
  0.6 133.8 %copy-start.2 = (f32[2,256,256]{2,1,0:T(8,128)S(1)}, f32[2,256,256]{2,1,0:T(8,128)}, u32[]{:S(2)}) copy-start(f32[2,256,256]{2,1,0:T(8,128)} %m1_hbm.1) | copy-start | bytes 1572868
  0.7 133.8 %copy-start.1 = (f32[2,256,256]{2,1,0:T(8,128)S(1)}, f32[2,256,256]{2,1,0:T(8,128)}, u32[]{:S(2)}) copy-start(f32[2,256,256]{2,1,0:T(8,128)} %ms_hbm.1) | copy-start | bytes 1572868
  134.4 4.9 %copy-start.4 = (bf16[256,256]{1,0:T(8,128)(2,1)S(1)}, bf16[256,256]{1,0:T(8,128)(2,1)}, u32[]{:S(2)}) copy-start(bf16[256,256]{1,0:T(8,128)(2,1)} %get-tuple-element.11) | copy-start | bytes 393220
  134.4 5.6 %copy-start = (bf16[2,16,8,32,256]{4,3,2,1,0:T(8,128)(2,1)S(1)}, bf16[2,16,8,32,256]{4,3,2,1,0:T(8,128)(2,1)}, u32[]{:S(2)}) copy-start(bf16[2,16,8,32,256]{4,3,2,1,0:T(8,128)(2,1)} %get-tuple-element.13) | copy-start | bytes 12582916

commit v4 on v3

--- a/solution.py
+++ b/solution.py
@@ -73,7 +73,7 @@
     xf_send_sem, xf_recv_sem, term_send_sem, term_recv_sem, kg_send_sem, kg_recv_sem,
     rs_send_sem, rs_recv_sem, ga_send_sem, ga_recv_sem,
     sw_send_sem, sw_recv_sem, ring_send_sem, ring_recv_sem,
-    zs_send_sem, zs_recv_sem, pl_send_sem, pl_recv_sem,
+    zs_send_sem, zs_recv_sem, s1_send_sem, s1_recv_sem, s2_send_sem, s2_recv_sem,
 ):
     c = lax.axis_index("ctx")
     d = lax.axis_index("dp")
@@ -157,7 +157,7 @@
             kv_send_sem.at[g, k - 1], kv_recv_sem.at[g, k - 1], ctx_peer(k),
         )
 
-    for k in range(1, BACK + 1):
+    for k in range(BACK, 0, -1):
         @pl.when(c + k < NCTX)
         def _(k=k):
             doc_copy(k).start()
@@ -312,7 +312,7 @@
             term_send[g, 0, k - 1] = (dk_acc[rows, :] * inv_root).astype(BF16)
             term_send[g, 1, k - 1] = dv_acc[rows, :].astype(BF16)
         for kind in range(2):
-            for k in range(1, BACK + 1):
+            for k in range(BACK, 0, -1):
                 @pl.when(c >= k)
                 def _(k=k, g=g, kind=kind):
                     term_copy(g, kind, k).start()
@@ -460,53 +460,70 @@
             ring_send_sem.at[way, s, int(same)], ring_recv_sem.at[way, s, int(same)], z_peer(step),
         )
 
-    def zs_start(k, carry):
-        zs_copy(k).start()
-        return carry
-
-    sent.append(swap.wait_send)
-    sent.append(lambda: over(1, NZ, lambda k: zs_copy(k).wait_send()))
+    over(1, NZ, lambda k: zs_copy(k).start())
     swap.start()
     ring_copy(0, 0, True, wb.at[0]).start()
     ring_copy(0, 1, True, wb.at[0]).start()
-    lax.fori_loop(1, NZ, zs_start, 0)
-
-    def zs_wait(k, carry):
-        zs_copy(k).wait_recv()
-        return carry
-
     swap.wait_recv()
     ring_copy(0, 0, False).start()
     ring_copy(0, 1, False).start()
-    lax.fori_loop(1, NZ, zs_wait, 0)
+    over(1, NZ, lambda k: zs_copy(k).wait_recv())
     for keep in keeps:
         keep.wait()
 
-    def pl_copy(k):
-        device = plane_peer(k)[1]
-        part = kw_hbm.at[1, pl.ds(xl * NZ, NZ), c]
-        return remote(part, part, pl_send_sem.at[k], pl_recv_sem.at[k], device)
-
-    def pl_start(k, carry):
-        pl_copy(k).start()
-        return carry
-
-    lax.fori_loop(1, NPLANE, pl_start, 0)
-
-    sent.append(lambda: over(1, NPLANE, lambda k: pl_copy(k).wait_send()))
+    y = c // 2
+    x = 2 * lax.rem(c, 2) + xl
+
+    def chip(xx, yy):
+        xx, yy = lax.rem(xx, 4), lax.rem(yy, 4)
+        return (2 * yy + xx // 2, lax.rem(xx, 2) * NZ + z, t)
+
+    def piece(xx, yy, first):
+        xx, yy = lax.rem(xx, 4), lax.rem(yy, 4)
+        return kw_hbm.at[1, pl.ds(lax.rem(xx, 2) * NZ + first * (NZ // 2), NZ // 2), 2 * yy + xx // 2]
+
+    def stage1(first, j):
+        part = piece(x, y, first)
+        device = chip(x + j, y) if first == 0 else chip(x, y + j)
+        return remote(part, part, s1_send_sem.at[first, j], s1_recv_sem.at[first, j], device)
+
+    def stage2(first, a, j):
+        part = piece(x + 4 - a, y, first) if first == 0 else piece(x, y + 4 - a, first)
+        device = chip(x, y + j) if first == 0 else chip(x + j, y)
+        return remote(part, part, s2_send_sem.at[first, a, j], s2_recv_sem.at[first, a, j], device)
+
     ring = [(s, way, same) for s in range(4) for same in (True, False) for way in range(2) if s < 3 or same == (way == 0)]
-    for s, way, same in ring:
-        ring_copy(s, way, same).wait_recv()
-        if (s + 1, way, same) in ring:
-            ring_copy(s + 1, way, same).start()
-
+
+    def ring_step(step):
+        for s, way, same in ring:
+            if s == step:
+                ring_copy(s, way, same).wait_recv()
+                if (s + 1, way, same) in ring:
+                    ring_copy(s + 1, way, same).start()
+
+    for j in (2, 1, 3):
+        for first in range(2):
+            stage1(first, j).start()
+    for j in (2, 1, 3):
+        for first in range(2):
+            stage2(first, 0, j).start()
+    ring_step(0)
+    for step, a in enumerate((1, 3, 2)):
+        for first in range(2):
+            stage1(first, a).wait_recv()
+            over(1, 4, lambda j: stage2(first, a, j).start())
+        ring_step(step + 1)
+    for first in range(2):
+        for a in range(4):
+            over(1, 4, lambda j: stage2(first, a, j).wait_recv())
+
+    sent.append(swap.wait_send)
+    sent.append(lambda: over(1, NZ, lambda k: zs_copy(k).wait_send()))
     sent.extend(ring_copy(s, way, same).wait_send for s, way, same in ring)
-
-    def pl_wait(k, carry):
-        pl_copy(k).wait_recv()
-        return carry
-
-    lax.fori_loop(1, NPLANE, pl_wait, 0)
+    for first in range(2):
+        sent.append(lambda first=first: over(1, 4, lambda j: stage1(first, j).wait_send()))
+        for a in range(4):
+            sent.append(lambda first=first, a=a: over(1, 4, lambda j: stage2(first, a, j).wait_send()))
 
     for wait in sent:
         wait()
@@ -576,7 +593,8 @@
             dma, dma,
             dma((2, 4, 2)), dma((2, 4, 2)),
             dma((NZ,)), dma((NZ,)),
-            dma((NPLANE,)), dma((NPLANE,)),
+            dma((2, 4)), dma((2, 4)),
+            dma((2, 4, 4)), dma((2, 4, 4)),
         ],
         compiler_params=pltpu.CompilerParams(
             collective_id=0, has_side_effects=True, vmem_limit_bytes=54 * 1024 * 1024

time: 143 us -> 136 us (0.951)
  Pallas kernels: 132 us -> 125 us
    pallas_call x1, Pallas kernels: 132 us -> 125 us  [on_device(): pl.pallas_call(kernel, out_shape=(jax.ShapeDtypeStruct((LOC, KVH * GROUP...]
where the time goes in v4:
time: 136 us
  Pallas kernels  125 us (92%)
  local copies, waits for them, and re-layouts  5 us (4%)
  other arithmetic  4.74 us (3%)
    pallas_call x1, Pallas kernels, on_device(): pl.pallas_call(kernel, out_shape=(jax.ShapeDtypeStruct((LOC, KVH * GROUP...  125 us
    unnamed x13, local copies, waits for them, and re-layouts  5 us

profile of v4, /device:TPU:8, one launch (start us, length us, event | category | flops | bytes accessed | tf_op | source)
XLA Modules:
  0.0 135.7 jit_solution(1289317973491747940)
XLA Ops:
  0.6 0.0 copy-start.3
  0.6 0.0 copy-start.2
  0.7 0.0 copy-start.1
  0.7 0.8 add_multiply_fusion
  1.5 0.6 fusion.3
  2.0 0.8 pad_maximum_fusion
  2.9 125.2 %shard_map.145 = (bf16[256,2048]{1,0:T(8,128)(2,1)}, bf16[256,256]{1,0:T(8,128)(2,1)}, f32[2,256,256]{2,1,0:T(8,128)}, bf16[2,16,8,32,256]{4,3,2,1,0:T(8,128)(2,1)}) custom-call(bf16[256,2048]{1,0:T(8,128)(2,1)} %bitcast.11, bf16[256,2048]{1,0:T(8,128)(2,1)} %bitcast.12, bf16[256,256]{1,0:T(8,128)(2,1)} %bitcast.14, bf16[256,256]{1,0:T(8,128)(2,1)} %bitcast.15, ...), custom_call_target="tpu_custom_call" | custom-call | tf_op jit(solution)/shard_map/pallas_call | solution.py:547
  128.1 0.0 copy-start.4
  128.1 0.0 copy-start
  128.1 0.0 copy-done.3
  128.1 0.0 copy-done.2
  128.1 0.0 copy-done.1
  128.1 2.6 %multiply_subtract_fusion = (f32[2,256,256]{2,1,0:T(8,128)}, f32[2,256,256]{2,1,0:T(8,128)}, f32[2,256,256]{2,1,0:T(8,128)}) fusion(f32[2,256,256]{2,1,0:T(8,128)S(1)} %copy-done.1, f32[2,256,256]{2,1,0:T(8,128)} %get-tuple-element.12, f32[2,256,256]{2,1,0:T(8,128)S(1)} %copy-done.2, f32[2,256,256]{2,1,0:T(8,128)S(1)} %copy-done.3), kind=kLoop, calls=%fused_computation.2 | loop fusion | flops 1966080 | bytes 3670016 | tf_op jit(solution)/shard_map/sub | solution.py:60
  130.7 2.3 %copy.19 = bf16[1,256,2048]{2,1,0:T(8,128)(2,1)} copy(bf16[1,256,2048]{2,1,0:T(8,128)(2,1)} %bitcast.10) | data formatting | bytes 2097152
  133.0 0.0 copy-done.4
  133.0 0.7 copy.20
  133.7 0.0 copy-done
  133.7 2.0 %copy.21 = bf16[2,4096,256]{2,1,0:T(8,128)(2,1)} copy(bf16[2,4096,256]{2,1,0:T(8,128)(2,1)S(1)} %bitcast.8) | data formatting | bytes 8388608
  (1 shorter events, 0.0 us)
Async XLA Ops:
  0.6 127.5 %copy-start.3 = (f32[2,256,256]{2,1,0:T(8,128)S(1)}, f32[2,256,256]{2,1,0:T(8,128)}, u32[]{:S(2)}) copy-start(f32[2,256,256]{2,1,0:T(8,128)} %m2_hbm.1) | copy-start | bytes 1572868
  0.6 127.5 %copy-start.2 = (f32[2,256,256]{2,1,0:T(8,128)S(1)}, f32[2,256,256]{2,1,0:T(8,128)}, u32[]{:S(2)}) copy-start(f32[2,256,256]{2,1,0:T(8,128)} %m1_hbm.1) | copy-start | bytes 1572868
  0.7 127.5 %copy-start.1 = (f32[2,256,256]{2,1,0:T(8,128)S(1)}, f32[2,256,256]{2,1,0:T(8,128)}, u32[]{:S(2)}) copy-start(f32[2,256,256]{2,1,0:T(8,128)} %ms_hbm.1) | copy-start | bytes 1572868
  128.1 4.9 %copy-start.4 = (bf16[256,256]{1,0:T(8,128)(2,1)S(1)}, bf16[256,256]{1,0:T(8,128)(2,1)}, u32[]{:S(2)}) copy-start(bf16[256,256]{1,0:T(8,128)(2,1)} %get-tuple-element.11) | copy-start | bytes 393220
  128.1 5.6 %copy-start = (bf16[2,16,8,32,256]{4,3,2,1,0:T(8,128)(2,1)S(1)}, bf16[2,16,8,32,256]{4,3,2,1,0:T(8,128)(2,1)}, u32[]{:S(2)}) copy-start(bf16[2,16,8,32,256]{4,3,2,1,0:T(8,128)(2,1)} %get-tuple-element.13) | copy-start | bytes 12582916

commit v5 on v4

--- a/solution.py
+++ b/solution.py
@@ -245,6 +245,35 @@
 
     sent.append(lambda: term_sent(0))
     sent.append(lambda: term_sent(1))
+    def kg_copy(s, way, g):
+        zb = lax.rem(z + (NZ - s if way == 0 else s), NZ)
+        part = kgt.at[zb, pl.ds(g * HD, HD), :]
+        return remote(
+            part, part, kg_send_sem.at[way, s, g], kg_recv_sem.at[way, s, g],
+            z_peer(1 if way == 0 else NZ - 1),
+        )
+
+    kg_ring = [(s, way, g) for s in range(4) for g in range(KVH) for way in range(2) if s < 3 or g == way]
+
+    def key_gradient(g):
+        for k in range(1, BACK + 1):
+            @pl.when(c + k < NCTX)
+            def _(k=k):
+                term_copy(g, 0, k).wait_recv()
+                kg_own[g] = kg_own[g] + term_recv[g, 0, k - 1].astype(F32)
+        kg = kg_own[g]
+        kg = kg * cos_ref[...] - pltpu.roll(kg, HD // 2, 1) * sin_ref[...]
+        kgt[z, pl.ds(g * HD, HD), :] = kg.T.astype(BF16)
+        for way in range(2):
+            kg_copy(0, way, g).start()
+
+    def kg_step(step, head):
+        for s, way, g in kg_ring:
+            if s == step and g == head:
+                kg_copy(s, way, g).wait_recv()
+                if (s + 1, way, g) in kg_ring:
+                    kg_copy(s + 1, way, g).start()
+
     for g in range(KVH):
         for k in range(1, BACK + 1):
             @pl.when(c >= k)
@@ -294,13 +323,17 @@
             dq = dq * cos_ref[...] - pltpu.roll(dq, HD // 2, 1) * sin_ref[...]
             dq_v[:, head_columns(h)] = dq.astype(BF16)
 
-        def two_heads(i, carry):
+        def two_heads(i, carry, g=g):
             for b in range(2):
                 products(2 * i + b, b)
             for b in range(2):
                 softmax(b)
             for b in range(2):
                 gradients(2 * i + b, b)
+            if g == 1:
+                pl.when(i == 1)(lambda: key_gradient(0))
+                pl.when(i == 2)(lambda: kg_step(0, 0))
+                pl.when(i == 3)(lambda: kg_step(1, 0))
             return carry
 
         lax.fori_loop(0, GROUP // 2, two_heads, 0)
@@ -321,26 +354,8 @@
     dq_copy.start()
     sent.append(dq_copy.wait)
 
-    def kg_copy(s, way, g):
-        zb = lax.rem(z + (NZ - s if way == 0 else s), NZ)
-        part = kgt.at[zb, pl.ds(g * HD, HD), :]
-        return remote(
-            part, part, kg_send_sem.at[way, s, g], kg_recv_sem.at[way, s, g],
-            z_peer(1 if way == 0 else NZ - 1),
-        )
-
-    kg_ring = [(s, way, g) for s in range(4) for g in range(KVH) for way in range(2) if s < 3 or g == way]
-    for g in range(KVH):
-        for k in range(1, BACK + 1):
-            @pl.when(c + k < NCTX)
-            def _(k=k, g=g):
-                term_copy(g, 0, k).wait_recv()
-                kg_own[g] = kg_own[g] + term_recv[g, 0, k - 1].astype(F32)
-        kg = kg_own[g]
-        kg = kg * cosv - pltpu.roll(kg, HD // 2, 1) * sinv
-        kgt[z, pl.ds(g * HD, HD), :] = kg.T.astype(BF16)
-        for way in range(2):
-            kg_copy(0, way, g).start()
+    kg_step(2, 0)
+    key_gradient(1)
 
     def xf_copy(k):
         rows = pl.ds(pl.multiple_of(lax.rem(z + NZ - k, NZ) * LOC, LOC), LOC)
@@ -356,18 +371,10 @@
             x_copy(k, 1).wait_recv()
         xf_copy(k).start()
 
-    for g in range(KVH):
-        for k in range(1, BACK + 1):
-            @pl.when(c + k < NCTX)
-            def _(k=k, g=g):
-                term_copy(g, 1, k).wait_recv()
-                dv_own[g] = dv_own[g] + term_recv[g, 1, k - 1].astype(F32)
-        dv_out[:, g * HD:(g + 1) * HD] = dv_own[g].astype(BF16)
-
-    for s, way, g in kg_ring:
-        kg_copy(s, way, g).wait_recv()
-        if (s + 1, way, g) in kg_ring:
-            kg_copy(s + 1, way, g).start()
+    for step in range(3):
+        kg_step(step, 1)
+    kg_step(3, 0)
+    kg_step(3, 1)
     sources = (0, 1, 7, 2, 6, 3, 5, 4)
     x_forward(sources[0])
     sent.extend(kg_copy(s, way, g).wait_send for s, way, g in kg_ring)
@@ -404,6 +411,14 @@
         return carry
 
     lax.fori_loop(1, NPLANE, rs_start, 0)
+
+    for g in range(KVH):
+        for k in range(1, BACK + 1):
+            @pl.when(c + k < NCTX)
+            def _(k=k, g=g):
+                term_copy(g, 1, k).wait_recv()
+                dv_own[g] = dv_own[g] + term_recv[g, 1, k - 1].astype(F32)
+        dv_out[:, g * HD:(g + 1) * HD] = dv_own[g].astype(BF16)
 
     def rs_sum(k, total):
         rs_copy(k).wait_recv()

time: 136 us -> 150 us (1.10)
  Pallas kernels: 125 us -> 140 us
    pallas_call x1, Pallas kernels: 125 us -> 140 us  [on_device(): pl.pallas_call(kernel, out_shape=(jax.ShapeDtypeStruct((LOC, KVH * GROUP...]
where the time goes in v5:
time: 150 us
  Pallas kernels  140 us (93%)
  local copies, waits for them, and re-layouts  5 us (3%)
  other arithmetic  4.74 us (3%)
    pallas_call x1, Pallas kernels, on_device(): pl.pallas_call(kernel, out_shape=(jax.ShapeDtypeStruct((LOC, KVH * GROUP...  140 us
    unnamed x13, local copies, waits for them, and re-layouts  5 us

profile of v5, /device:TPU:8, one launch (start us, length us, event | category | flops | bytes accessed | tf_op | source)
XLA Modules:
  0.0 150.3 jit_solution(6754344724707754141)
XLA Ops:
  0.6 0.0 copy-start.3
  0.6 0.0 copy-start.2
  0.7 0.0 copy-start.1
  0.7 0.8 add_multiply_fusion
  1.5 0.6 fusion.3
  2.0 0.8 pad_maximum_fusion
  2.9 139.9 %shard_map.145 = (bf16[256,2048]{1,0:T(8,128)(2,1)}, bf16[256,256]{1,0:T(8,128)(2,1)}, f32[2,256,256]{2,1,0:T(8,128)}, bf16[2,16,8,32,256]{4,3,2,1,0:T(8,128)(2,1)}) custom-call(bf16[256,2048]{1,0:T(8,128)(2,1)} %bitcast.11, bf16[256,2048]{1,0:T(8,128)(2,1)} %bitcast.12, bf16[256,256]{1,0:T(8,128)(2,1)} %bitcast.14, bf16[256,256]{1,0:T(8,128)(2,1)} %bitcast.15, ...), custom_call_target="tpu_custom_call" | custom-call | tf_op jit(solution)/shard_map/pallas_call | solution.py:562
  142.7 0.0 copy-start.4
  142.7 0.0 copy-start
  142.7 0.0 copy-done.3
  142.8 0.0 copy-done.2
  142.8 0.0 copy-done.1
  142.8 2.6 %multiply_subtract_fusion = (f32[2,256,256]{2,1,0:T(8,128)}, f32[2,256,256]{2,1,0:T(8,128)}, f32[2,256,256]{2,1,0:T(8,128)}) fusion(f32[2,256,256]{2,1,0:T(8,128)S(1)} %copy-done.1, f32[2,256,256]{2,1,0:T(8,128)} %get-tuple-element.12, f32[2,256,256]{2,1,0:T(8,128)S(1)} %copy-done.2, f32[2,256,256]{2,1,0:T(8,128)S(1)} %copy-done.3), kind=kLoop, calls=%fused_computation.2 | loop fusion | flops 1966080 | bytes 3670016 | tf_op jit(solution)/shard_map/sub | solution.py:60
  145.3 2.3 %copy.19 = bf16[1,256,2048]{2,1,0:T(8,128)(2,1)} copy(bf16[1,256,2048]{2,1,0:T(8,128)(2,1)} %bitcast.10) | data formatting | bytes 2097152
  147.7 0.0 copy-done.4
  147.7 0.7 copy.20
  148.3 0.0 copy-done
  148.3 2.0 %copy.21 = bf16[2,4096,256]{2,1,0:T(8,128)(2,1)} copy(bf16[2,4096,256]{2,1,0:T(8,128)(2,1)S(1)} %bitcast.8) | data formatting | bytes 8388608
  (1 shorter events, 0.0 us)
Async XLA Ops:
  0.6 142.1 %copy-start.3 = (f32[2,256,256]{2,1,0:T(8,128)S(1)}, f32[2,256,256]{2,1,0:T(8,128)}, u32[]{:S(2)}) copy-start(f32[2,256,256]{2,1,0:T(8,128)} %m2_hbm.1) | copy-start | bytes 1572868
  0.6 142.1 %copy-start.2 = (f32[2,256,256]{2,1,0:T(8,128)S(1)}, f32[2,256,256]{2,1,0:T(8,128)}, u32[]{:S(2)}) copy-start(f32[2,256,256]{2,1,0:T(8,128)} %m1_hbm.1) | copy-start | bytes 1572868
  0.7 142.1 %copy-start.1 = (f32[2,256,256]{2,1,0:T(8,128)S(1)}, f32[2,256,256]{2,1,0:T(8,128)}, u32[]{:S(2)}) copy-start(f32[2,256,256]{2,1,0:T(8,128)} %ms_hbm.1) | copy-start | bytes 1572868
  142.7 4.9 %copy-start.4 = (bf16[256,256]{1,0:T(8,128)(2,1)S(1)}, bf16[256,256]{1,0:T(8,128)(2,1)}, u32[]{:S(2)}) copy-start(bf16[256,256]{1,0:T(8,128)(2,1)} %get-tuple-element.11) | copy-start | bytes 393220
  142.7 5.6 %copy-start = (bf16[2,16,8,32,256]{4,3,2,1,0:T(8,128)(2,1)S(1)}, bf16[2,16,8,32,256]{4,3,2,1,0:T(8,128)(2,1)}, u32[]{:S(2)}) copy-start(bf16[2,16,8,32,256]{4,3,2,1,0:T(8,128)(2,1)} %get-tuple-element.13) | copy-start | bytes 12582916

commit v6 on v5

--- a/solution.py
+++ b/solution.py
@@ -235,6 +235,12 @@
             term_send_sem.at[g, kind, k - 1], term_recv_sem.at[g, kind, k - 1],
             ctx_peer(NCTX - k),
         )
+
+    def term_start(g, kind):
+        for k in range(BACK, 0, -1):
+            @pl.when(c >= k)
+            def _(k=k):
+                term_copy(g, kind, k).start()
 
     def term_sent(g):
         for k in range(1, BACK + 1):
@@ -330,10 +336,6 @@
                 softmax(b)
             for b in range(2):
                 gradients(2 * i + b, b)
-            if g == 1:
-                pl.when(i == 1)(lambda: key_gradient(0))
-                pl.when(i == 2)(lambda: kg_step(0, 0))
-                pl.when(i == 3)(lambda: kg_step(1, 0))
             return carry
 
         lax.fori_loop(0, GROUP // 2, two_heads, 0)
@@ -344,18 +346,20 @@
             rows = slice(k * LOC, (k + 1) * LOC)
             term_send[g, 0, k - 1] = (dk_acc[rows, :] * inv_root).astype(BF16)
             term_send[g, 1, k - 1] = dv_acc[rows, :].astype(BF16)
-        for kind in range(2):
-            for k in range(BACK, 0, -1):
-                @pl.when(c >= k)
-                def _(k=k, g=g, kind=kind):
-                    term_copy(g, kind, k).start()
+        term_start(g, 0)
+        if g == 0:
+            term_start(g, 1)
 
     dq_copy = pltpu.make_async_copy(dq_v, dq_hbm, local_sem.at[7])
     dq_copy.start()
     sent.append(dq_copy.wait)
 
+    key_gradient(0)
+    kg_step(0, 0)
+    kg_step(1, 0)
+    key_gradient(1)
+    term_start(1, 1)
     kg_step(2, 0)
-    key_gradient(1)
 
     def xf_copy(k):
         rows = pl.ds(pl.multiple_of(lax.rem(z + NZ - k, NZ) * LOC, LOC), LOC)

time: 150 us -> 142 us (0.947)
  Pallas kernels: 140 us -> 131 us
    pallas_call x1, Pallas kernels: 140 us -> 131 us  [on_device(): pl.pallas_call(kernel, out_shape=(jax.ShapeDtypeStruct((LOC, KVH * GROUP...]
where the time goes in v6:
time: 142 us; the launch traced here: 141 us
  Pallas kernels  131 us (92%)
  local copies, waits for them, and re-layouts  5 us (4%)
  other arithmetic  4.74 us (3%)
    pallas_call x1, Pallas kernels, on_device(): pl.pallas_call(kernel, out_shape=(jax.ShapeDtypeStruct((LOC, KVH * GROUP...  131 us
    unnamed x13, local copies, waits for them, and re-layouts  5 us

profile of v6, /device:TPU:8, one launch (start us, length us, event | category | flops | bytes accessed | tf_op | source)
XLA Modules:
  0.0 141.3 jit_solution(1814087608520567824)
XLA Ops:
  0.6 0.0 copy-start.3
  0.6 0.0 copy-start.2
  0.7 0.0 copy-start.1
  0.7 0.8 add_multiply_fusion
  1.5 0.6 fusion.3
  2.0 0.8 pad_maximum_fusion
  2.9 130.8 %shard_map.145 = (bf16[256,2048]{1,0:T(8,128)(2,1)}, bf16[256,256]{1,0:T(8,128)(2,1)}, f32[2,256,256]{2,1,0:T(8,128)}, bf16[2,16,8,32,256]{4,3,2,1,0:T(8,128)(2,1)}) custom-call(bf16[256,2048]{1,0:T(8,128)(2,1)} %bitcast.11, bf16[256,2048]{1,0:T(8,128)(2,1)} %bitcast.12, bf16[256,256]{1,0:T(8,128)(2,1)} %bitcast.14, bf16[256,256]{1,0:T(8,128)(2,1)} %bitcast.15, ...), custom_call_target="tpu_custom_call" | custom-call | tf_op jit(solution)/shard_map/pallas_call | solution.py:566
  133.7 0.0 copy-start.4
  133.7 0.0 copy-start
  133.7 0.0 copy-done.3
  133.7 0.0 copy-done.2
  133.7 0.0 copy-done.1
  133.8 2.6 %multiply_subtract_fusion = (f32[2,256,256]{2,1,0:T(8,128)}, f32[2,256,256]{2,1,0:T(8,128)}, f32[2,256,256]{2,1,0:T(8,128)}) fusion(f32[2,256,256]{2,1,0:T(8,128)S(1)} %copy-done.1, f32[2,256,256]{2,1,0:T(8,128)} %get-tuple-element.12, f32[2,256,256]{2,1,0:T(8,128)S(1)} %copy-done.2, f32[2,256,256]{2,1,0:T(8,128)S(1)} %copy-done.3), kind=kLoop, calls=%fused_computation.2 | loop fusion | flops 1966080 | bytes 3670016 | tf_op jit(solution)/shard_map/sub | solution.py:60
  136.3 2.3 %copy.19 = bf16[1,256,2048]{2,1,0:T(8,128)(2,1)} copy(bf16[1,256,2048]{2,1,0:T(8,128)(2,1)} %bitcast.10) | data formatting | bytes 2097152
  138.6 0.0 copy-done.4
  138.6 0.7 copy.20
  139.3 0.0 copy-done
  139.3 2.0 %copy.21 = bf16[2,4096,256]{2,1,0:T(8,128)(2,1)} copy(bf16[2,4096,256]{2,1,0:T(8,128)(2,1)S(1)} %bitcast.8) | data formatting | bytes 8388608
  (1 shorter events, 0.0 us)
Async XLA Ops:
  0.6 133.1 %copy-start.3 = (f32[2,256,256]{2,1,0:T(8,128)S(1)}, f32[2,256,256]{2,1,0:T(8,128)}, u32[]{:S(2)}) copy-start(f32[2,256,256]{2,1,0:T(8,128)} %m2_hbm.1) | copy-start | bytes 1572868
  0.6 133.1 %copy-start.2 = (f32[2,256,256]{2,1,0:T(8,128)S(1)}, f32[2,256,256]{2,1,0:T(8,128)}, u32[]{:S(2)}) copy-start(f32[2,256,256]{2,1,0:T(8,128)} %m1_hbm.1) | copy-start | bytes 1572868
  0.7 133.1 %copy-start.1 = (f32[2,256,256]{2,1,0:T(8,128)S(1)}, f32[2,256,256]{2,1,0:T(8,128)}, u32[]{:S(2)}) copy-start(f32[2,256,256]{2,1,0:T(8,128)} %ms_hbm.1) | copy-start | bytes 1572868
  133.7 4.9 %copy-start.4 = (bf16[256,256]{1,0:T(8,128)(2,1)S(1)}, bf16[256,256]{1,0:T(8,128)(2,1)}, u32[]{:S(2)}) copy-start(bf16[256,256]{1,0:T(8,128)(2,1)} %get-tuple-element.11) | copy-start | bytes 393220
  133.7 5.6 %copy-start = (bf16[2,16,8,32,256]{4,3,2,1,0:T(8,128)(2,1)S(1)}, bf16[2,16,8,32,256]{4,3,2,1,0:T(8,128)(2,1)}, u32[]{:S(2)}) copy-start(bf16[2,16,8,32,256]{4,3,2,1,0:T(8,128)(2,1)} %get-tuple-element.13) | copy-start | bytes 12582916

commit v7 on v4

--- a/solution.py
+++ b/solution.py
@@ -321,15 +321,10 @@
     dq_copy.start()
     sent.append(dq_copy.wait)
 
-    def kg_copy(s, way, g):
-        zb = lax.rem(z + (NZ - s if way == 0 else s), NZ)
-        part = kgt.at[zb, pl.ds(g * HD, HD), :]
-        return remote(
-            part, part, kg_send_sem.at[way, s, g], kg_recv_sem.at[way, s, g],
-            z_peer(1 if way == 0 else NZ - 1),
-        )
-
-    kg_ring = [(s, way, g) for s in range(4) for g in range(KVH) for way in range(2) if s < 3 or g == way]
+    def kg_copy(k, g):
+        part = kgt.at[z, pl.ds(g * HD, HD), :]
+        return remote(part, part, kg_send_sem.at[k, g], kg_recv_sem.at[k, g], z_peer(k))
+
     for g in range(KVH):
         for k in range(1, BACK + 1):
             @pl.when(c + k < NCTX)
@@ -339,8 +334,8 @@
         kg = kg_own[g]
         kg = kg * cosv - pltpu.roll(kg, HD // 2, 1) * sinv
         kgt[z, pl.ds(g * HD, HD), :] = kg.T.astype(BF16)
-        for way in range(2):
-            kg_copy(0, way, g).start()
+        for k in (4, 3, 5, 2, 6, 1, 7):
+            kg_copy(k, g).start()
 
     def xf_copy(k):
         rows = pl.ds(pl.multiple_of(lax.rem(z + NZ - k, NZ) * LOC, LOC), LOC)
@@ -364,18 +359,18 @@
                 dv_own[g] = dv_own[g] + term_recv[g, 1, k - 1].astype(F32)
         dv_out[:, g * HD:(g + 1) * HD] = dv_own[g].astype(BF16)
 
-    for s, way, g in kg_ring:
-        kg_copy(s, way, g).wait_recv()
-        if (s + 1, way, g) in kg_ring:
-            kg_copy(s + 1, way, g).start()
     sources = (0, 1, 7, 2, 6, 3, 5, 4)
     x_forward(sources[0])
-    sent.extend(kg_copy(s, way, g).wait_send for s, way, g in kg_ring)
+    for g in range(KVH):
+        sent.append(lambda g=g: over(1, NZ, lambda k: kg_copy(k, g).wait_send()))
     sent.append(lambda: over(0, NZ, lambda k: xf_copy(k).wait_send()))
 
     for n, k in enumerate(sources):
         if n + 1 < NZ:
             x_forward(sources[n + 1])
+        for g in range(KVH):
+            if k > 0:
+                kg_copy(k, g).wait_recv()
         xf_copy(k).wait_recv()
         source = lax.rem(z + NZ - k, NZ)
         tokens = pl.ds(pl.multiple_of(source * LOC, LOC), LOC)
@@ -587,7 +582,7 @@
             dma((NZ, 2)), dma((NZ, 2)),
             dma((NZ,)), dma((NZ,)),
             dma((KVH, 2, BACK)), dma((KVH, 2, BACK)),
-            dma((2, 4, KVH)), dma((2, 4, KVH)),
+            dma((NZ, KVH)), dma((NZ, KVH)),
             dma((NPLANE,)), dma((NPLANE,)),
             dma((NCTX,)), dma((NCTX,)),
             dma, dma,

time: 136 us -> 143 us (1.051)
  Pallas kernels: 125 us -> 132 us
    pallas_call x1, Pallas kernels: 125 us -> 132 us  [on_device(): pl.pallas_call(kernel, out_shape=(jax.ShapeDtypeStruct((LOC, KVH * GROUP...]
where the time goes in v7:
time: 143 us; the launch traced here: 142 us
  Pallas kernels  132 us (92%)
  local copies, waits for them, and re-layouts  5 us (3%)
  other arithmetic  4.74 us (3%)
    pallas_call x1, Pallas kernels, on_device(): pl.pallas_call(kernel, out_shape=(jax.ShapeDtypeStruct((LOC, KVH * GROUP...  132 us
    unnamed x13, local copies, waits for them, and re-layouts  5 us

profile of v7, /device:TPU:8, one launch (start us, length us, event | category | flops | bytes accessed | tf_op | source)
XLA Modules:
  0.0 142.4 jit_solution(14075544640094554259)
XLA Ops:
  0.6 0.0 copy-start.3
  0.6 0.0 copy-start.2
  0.7 0.0 copy-start.1
  0.7 0.8 add_multiply_fusion
  1.5 0.6 fusion.3
  2.0 0.8 pad_maximum_fusion
  2.9 131.9 %shard_map.145 = (bf16[256,2048]{1,0:T(8,128)(2,1)}, bf16[256,256]{1,0:T(8,128)(2,1)}, f32[2,256,256]{2,1,0:T(8,128)}, bf16[2,16,8,32,256]{4,3,2,1,0:T(8,128)(2,1)}) custom-call(bf16[256,2048]{1,0:T(8,128)(2,1)} %bitcast.11, bf16[256,2048]{1,0:T(8,128)(2,1)} %bitcast.12, bf16[256,256]{1,0:T(8,128)(2,1)} %bitcast.14, bf16[256,256]{1,0:T(8,128)(2,1)} %bitcast.15, ...), custom_call_target="tpu_custom_call" | custom-call | tf_op jit(solution)/shard_map/pallas_call | solution.py:542
  134.8 0.0 copy-start.4
  134.8 0.0 copy-start
  134.8 0.0 copy-done.3
  134.8 0.0 copy-done.2
  134.8 0.0 copy-done.1
  134.8 2.6 %multiply_subtract_fusion = (f32[2,256,256]{2,1,0:T(8,128)}, f32[2,256,256]{2,1,0:T(8,128)}, f32[2,256,256]{2,1,0:T(8,128)}) fusion(f32[2,256,256]{2,1,0:T(8,128)S(1)} %copy-done.1, f32[2,256,256]{2,1,0:T(8,128)} %get-tuple-element.12, f32[2,256,256]{2,1,0:T(8,128)S(1)} %copy-done.2, f32[2,256,256]{2,1,0:T(8,128)S(1)} %copy-done.3), kind=kLoop, calls=%fused_computation.2 | loop fusion | flops 1966080 | bytes 3670016 | tf_op jit(solution)/shard_map/sub | solution.py:60
  137.4 2.3 %copy.19 = bf16[1,256,2048]{2,1,0:T(8,128)(2,1)} copy(bf16[1,256,2048]{2,1,0:T(8,128)(2,1)} %bitcast.10) | data formatting | bytes 2097152
  139.7 0.0 copy-done.4
  139.7 0.7 copy.20
  140.4 0.0 copy-done
  140.4 2.0 %copy.21 = bf16[2,4096,256]{2,1,0:T(8,128)(2,1)} copy(bf16[2,4096,256]{2,1,0:T(8,128)(2,1)S(1)} %bitcast.8) | data formatting | bytes 8388608
  (1 shorter events, 0.0 us)
Async XLA Ops:
  0.6 134.2 %copy-start.3 = (f32[2,256,256]{2,1,0:T(8,128)S(1)}, f32[2,256,256]{2,1,0:T(8,128)}, u32[]{:S(2)}) copy-start(f32[2,256,256]{2,1,0:T(8,128)} %m2_hbm.1) | copy-start | bytes 1572868
  0.6 134.2 %copy-start.2 = (f32[2,256,256]{2,1,0:T(8,128)S(1)}, f32[2,256,256]{2,1,0:T(8,128)}, u32[]{:S(2)}) copy-start(f32[2,256,256]{2,1,0:T(8,128)} %m1_hbm.1) | copy-start | bytes 1572868
  0.7 134.2 %copy-start.1 = (f32[2,256,256]{2,1,0:T(8,128)S(1)}, f32[2,256,256]{2,1,0:T(8,128)}, u32[]{:S(2)}) copy-start(f32[2,256,256]{2,1,0:T(8,128)} %ms_hbm.1) | copy-start | bytes 1572868
  134.8 4.9 %copy-start.4 = (bf16[256,256]{1,0:T(8,128)(2,1)S(1)}, bf16[256,256]{1,0:T(8,128)(2,1)}, u32[]{:S(2)}) copy-start(bf16[256,256]{1,0:T(8,128)(2,1)} %get-tuple-element.11) | copy-start | bytes 393220
  134.8 5.6 %copy-start = (bf16[2,16,8,32,256]{4,3,2,1,0:T(8,128)(2,1)S(1)}, bf16[2,16,8,32,256]{4,3,2,1,0:T(8,128)(2,1)}, u32[]{:S(2)}) copy-start(bf16[2,16,8,32,256]{4,3,2,1,0:T(8,128)(2,1)} %get-tuple-element.13) | copy-start | bytes 12582916
